TPU v7x, 128 devices: a whole 4x4x4 slice. The times are simulated.
128 devices in a mesh: dp: 2 (over y_lo), expert: 8 (over z, core), seq: 8 (over y_hi, x).
Axes of the slice: x: 4, y: 4 (y_hi: 2, y_lo: 2; y = y_hi * 2 + y_lo), z: 4, core: 2. Of those that a mesh axis runs over, the one named last changes fastest.
Arguments:
- attn_query: bfloat16 [32768, 2048], P(('dp', 'expert', 'seq')), may hold values from -5 to 5
- attn_key: bfloat16 [32768, 2048], P(('dp', 'expert', 'seq')), may hold values from -5 to 5
- attn_value: bfloat16 [32768, 2048], P(('dp', 'expert', 'seq')), may hold values from -5 to 5
- moe_input: bfloat16 [32768, 2048], P(('dp', 'expert', 'seq')), may hold values from -6 to 6
- cotangent: bfloat16 [32768, 2048], P(('dp', 'expert', 'seq')), may hold values from -6 to 6
- routes: int32 [32768, 2], P(('dp', 'expert', 'seq')), may hold values from 0 to 7, all different within a row; in each aligned block of 256 rows (0 to 255, 256 to 511, ...) at most 128 rows name the same one
- route_weight: bfloat16 [32768, 2], P(('dp', 'expert', 'seq')), may hold values from 0.099609375 to 1
- w_gate: bfloat16 [8, 2048, 512], P('expert'), may hold values from -0.125 to 0.125
- w_up: bfloat16 [8, 2048, 512], P('expert'), may hold values from -0.125 to 0.125
- w_down: bfloat16 [8, 512, 2048], P('expert'), may hold values from -0.25 to 0.25
Outputs:
- grad_hidden: bfloat16 [32768, 2048], P(('dp', 'expert', 'seq'))
- grad_query: bfloat16 [32768, 2048], P(('dp', 'expert', 'seq'))
- grad_key: bfloat16 [32768, 2048], P(('dp', 'expert', 'seq'))
- grad_value: bfloat16 [32768, 2048], P(('dp', 'expert', 'seq'))
- grad_gate: bfloat16 [8, 2048, 512], P('expert')
- grad_up: bfloat16 [8, 2048, 512], P('expert')
- grad_down: bfloat16 [8, 512, 2048], P('expert')
Inputs may be any that keep to these rules, and one draw needn't show every extreme that they name: `routes`: in the rows of one device no expert is named by more than 128 rows; a row names 2 different experts.
All inputs are finite; a program needn't handle non-finite values.
Results may differ from a plain program's by a relative error of at most 0.02.
Values may be sent and summed in bfloat16 or wider, within the bound.
A program may use at most 192 MiB of HBM per device.

v0:
```python
import jax
import jax.numpy as jnp
from jax import lax
from jax.sharding import PartitionSpec as P

TOP = 2
HD = 128


def slot_index(taken_rows, weight_rows, most_slots):
    place_rank = jnp.cumsum(taken_rows, axis=1) - 1
    slot_ids = jnp.arange(most_slots, dtype=jnp.int32)
    matched = (place_rank[:, None, :] == slot_ids[None, :, None]) & (taken_rows[:, None, :] > 0)
    positions = jnp.arange(taken_rows.shape[1], dtype=jnp.int32)
    row_index = jnp.sum(jnp.where(matched, positions[None, None, :], 0), axis=2)
    slot_weight = jnp.sum(jnp.where(matched, weight_rows[:, None, :], jnp.float32(0.0)), axis=2)
    return (row_index, slot_weight)


def expert_backward(rows_in, slot_weight, rows_grad, gate_matrix, up_matrix, down_matrix):
    contract_last = (((1,), (1,)), ((), ()))
    contract_first = (((0,), (0,)), ((), ()))
    gate_value = jnp.dot(rows_in, gate_matrix, preferred_element_type=jnp.float32)
    up_value = jnp.dot(rows_in, up_matrix, preferred_element_type=jnp.float32)
    sigmoid_gate = jax.nn.sigmoid(gate_value)
    activated = gate_value * sigmoid_gate
    inner_value = (activated * up_value).astype(jnp.bfloat16)
    scaled_grad = (slot_weight[:, None] * rows_grad.astype(jnp.float32)).astype(jnp.bfloat16)
    grad_inner = lax.dot_general(
        scaled_grad, down_matrix, contract_last, preferred_element_type=jnp.float32
    )
    grad_gate_value = (
        grad_inner * up_value * sigmoid_gate * (1.0 + gate_value * (1.0 - sigmoid_gate))
    ).astype(jnp.bfloat16)
    grad_up_value = (grad_inner * activated).astype(jnp.bfloat16)
    back_sum = lax.dot_general(
        grad_gate_value, gate_matrix, contract_last, preferred_element_type=jnp.float32
    )
    back_sum = back_sum + lax.dot_general(
        grad_up_value, up_matrix, contract_last, preferred_element_type=jnp.float32
    )
    hidden_part = back_sum.astype(jnp.bfloat16)
    gate_part = lax.dot_general(
        rows_in, grad_gate_value, contract_first, preferred_element_type=jnp.float32
    )
    up_part = lax.dot_general(
        rows_in, grad_up_value, contract_first, preferred_element_type=jnp.float32
    )
    down_part = lax.dot_general(
        inner_value, scaled_grad, contract_first, preferred_element_type=jnp.float32
    )
    return (hidden_part, gate_part, up_part, down_part)


def rounded(part_sum):
    return lax.optimization_barrier(part_sum.astype(jnp.bfloat16)).astype(jnp.float32)


def attention_backward(head_query, head_key, head_value, head_grad):
    seq_len, lanes = head_query.shape
    head_count = lanes // HD
    query_all = head_query.reshape(seq_len, head_count, HD)
    key_all = head_key.reshape(seq_len, head_count, HD)
    value_all = head_value.reshape(seq_len, head_count, HD)
    grad_all = head_grad.reshape(seq_len, head_count, HD)
    block_rows = min(512, seq_len)
    scale_factor = jnp.float32(HD ** (-0.5))

    def step_block(block_id, carry):
        grad_q_all, grad_k_sum, grad_v_sum = carry
        start = block_id * block_rows
        query_blk = lax.dynamic_slice_in_dim(query_all, start, block_rows, 0)
        grad_blk = lax.dynamic_slice_in_dim(grad_all, start, block_rows, 0)
        scores = (
            jnp.einsum("qhd,khd->hqk", query_blk, key_all, preferred_element_type=jnp.float32)
            * scale_factor
        )
        row_max = jnp.max(scores, axis=2, keepdims=True)
        expo_scores = jnp.exp(scores - row_max)
        probs = expo_scores / jnp.sum(expo_scores, axis=2, keepdims=True)
        probs_b = probs.astype(jnp.bfloat16)
        grad_v_sum = grad_v_sum + jnp.einsum(
            "hqk,qhd->khd", probs_b, grad_blk, preferred_element_type=jnp.float32
        )
        grad_probs = jnp.einsum(
            "qhd,khd->hqk", grad_blk, value_all, preferred_element_type=jnp.float32
        )
        delta_sum = jnp.sum(probs * grad_probs, axis=2, keepdims=True)
        grad_scores = (probs * (grad_probs - delta_sum)).astype(jnp.bfloat16)
        grad_q_blk = (
            jnp.einsum("hqk,khd->qhd", grad_scores, key_all, preferred_element_type=jnp.float32)
            * scale_factor
        ).astype(jnp.bfloat16)
        grad_k_sum = (
            grad_k_sum
            + jnp.einsum("hqk,qhd->khd", grad_scores, query_blk, preferred_element_type=jnp.float32)
            * scale_factor
        )
        grad_q_all = lax.dynamic_update_slice_in_dim(grad_q_all, grad_q_blk, start, 0)
        return (grad_q_all, grad_k_sum, grad_v_sum)

    initial = (
        jnp.zeros((seq_len, head_count, HD), jnp.bfloat16),
        jnp.zeros((seq_len, head_count, HD), jnp.float32),
        jnp.zeros((seq_len, head_count, HD), jnp.float32),
    )
    grad_q_all, grad_k_sum, grad_v_sum = lax.fori_loop(
        0, seq_len // block_rows, step_block, initial
    )
    return (
        grad_q_all.reshape(seq_len, lanes),
        grad_k_sum.astype(jnp.bfloat16).reshape(seq_len, lanes),
        grad_v_sum.astype(jnp.bfloat16).reshape(seq_len, lanes),
    )


def shards(
    attn_query,
    attn_key,
    attn_value,
    moe_input,
    cotangent,
    routes,
    route_weight,
    w_gate,
    w_up,
    w_down,
):
    tok_rows, width = moe_input.shape
    experts_n = lax.axis_size("expert")
    expert_index = lax.axis_index("expert")
    most_slots = min(tok_rows, 2 * tok_rows * TOP // experts_n)
    head_query, head_key, head_value = (
        lax.all_to_all(attn_query, "seq", split_axis=1, concat_axis=0, tiled=True),
        lax.all_to_all(attn_key, "seq", split_axis=1, concat_axis=0, tiled=True),
        lax.all_to_all(attn_value, "seq", split_axis=1, concat_axis=0, tiled=True),
    )
    expert_ids = jnp.arange(experts_n, dtype=jnp.int32)
    hits = routes[:, :, None] == expert_ids[None, None, :]
    weight_table = jnp.sum(
        jnp.where(hits, route_weight.astype(jnp.float32)[:, :, None], jnp.float32(0.0)), axis=1
    )
    gate_matrix = w_gate[0]
    up_matrix = w_up[0]
    down_matrix = w_down[0]
    table_b = weight_table.astype(jnp.bfloat16)
    all_input, all_grad, all_table = (
        lax.all_gather(moe_input, "expert", axis=0, tiled=True),
        lax.all_gather(cotangent, "expert", axis=0, tiled=True),
        lax.all_gather(table_b, "expert", axis=0, tiled=True),
    )
    own_column = lax.dynamic_slice_in_dim(all_table, expert_index, 1, 1)[:, 0].astype(jnp.float32)
    own_column = own_column.reshape(experts_n, tok_rows)
    taken_rows = (own_column > 0.0).astype(jnp.int32)
    row_index, slot_weight = slot_index(taken_rows, own_column, most_slots)
    sources = jnp.arange(experts_n, dtype=jnp.int32)[:, None]
    rows_in = all_input.reshape(experts_n, tok_rows, width)[sources, row_index].reshape(-1, width)
    rows_grad = all_grad.reshape(experts_n, tok_rows, width)[sources, row_index].reshape(-1, width)
    hidden_part, gate_part, up_part, down_part = expert_backward(
        rows_in, slot_weight.reshape(-1), rows_grad, gate_matrix, up_matrix, down_matrix
    )
    terms = (
        jnp.zeros((experts_n, tok_rows, width), jnp.float32)
        .at[sources, row_index]
        .add(hidden_part.reshape(experts_n, most_slots, width).astype(jnp.float32))
    )
    routed_sum = lax.psum_scatter(
        terms.reshape(experts_n * tok_rows, width).astype(jnp.bfloat16),
        "expert",
        scatter_dimension=0,
        tiled=True,
    ).astype(jnp.float32)
    grad_hidden = (cotangent.astype(jnp.float32) + routed_sum).astype(jnp.bfloat16)
    sum_gate, sum_up, sum_down = (
        lax.psum(rounded(gate_part).astype(jnp.bfloat16), ("dp", "seq")).astype(jnp.float32),
        lax.psum(rounded(up_part).astype(jnp.bfloat16), ("dp", "seq")).astype(jnp.float32),
        lax.psum(rounded(down_part).astype(jnp.bfloat16), ("dp", "seq")).astype(jnp.float32),
    )
    groups_n = jnp.float32(lax.axis_size("dp") * lax.axis_size("seq"))
    grad_gate = (sum_gate / groups_n)[None].astype(jnp.bfloat16)
    grad_up = (sum_up / groups_n)[None].astype(jnp.bfloat16)
    grad_down = (sum_down / groups_n)[None].astype(jnp.bfloat16)
    head_grad = lax.all_to_all(grad_hidden, "seq", split_axis=1, concat_axis=0, tiled=True)
    grad_q_heads, grad_k_heads, grad_v_heads = attention_backward(
        head_query, head_key, head_value, head_grad
    )
    grad_query, grad_key, grad_value = (
        lax.all_to_all(grad_q_heads, "seq", split_axis=0, concat_axis=1, tiled=True),
        lax.all_to_all(grad_k_heads, "seq", split_axis=0, concat_axis=1, tiled=True),
        lax.all_to_all(grad_v_heads, "seq", split_axis=0, concat_axis=1, tiled=True),
    )
    return (grad_hidden, grad_query, grad_key, grad_value, grad_gate, grad_up, grad_down)


def solution(mesh):
    placed = (
        P(("dp", "expert", "seq"), None),
        P(("dp", "expert", "seq"), None),
        P(("dp", "expert", "seq"), None),
        P(("dp", "expert", "seq"), None),
        P(("dp", "expert", "seq"), None),
        P(("dp", "expert", "seq"), None),
        P(("dp", "expert", "seq"), None),
        P("expert", None, None),
        P("expert", None, None),
        P("expert", None, None),
    )
    return jax.shard_map(
        shards,
        mesh=mesh,
        in_specs=placed,
        out_specs=(
            P(("dp", "expert", "seq"), None),
            P(("dp", "expert", "seq"), None),
            P(("dp", "expert", "seq"), None),
            P(("dp", "expert", "seq"), None),
            P("expert", None, None),
            P("expert", None, None),
            P("expert", None, None),
        ),
        check_vma=False,
    )
```

profile of v0, /device:TPU:104, one launch (start us, length us, event | category | flops | bytes accessed | tf_op | source)
XLA Modules:
  0.0 526.1 jit_solution(11480292536753893735)
XLA Ops:
  10.1 12.8 %all_gather.9 = bf16[2048,8]{0,1:T(8,128)(2,1)S(1)} all-gather(bf16[256,8]{0,1:T(8,128)(2,1)S(1)} %select_reduce_fusion.2), channel_id=1, replica_groups=mesh['dp'=2,'expert'=8,'seq'=8] {'expert'}, dimensions={0}, use_global_device_ids=true | all-gather | bytes 36864 | tf_op jit(solution)/shard_map/all_gather | solution.py:150
  25.9 32.8 %all-gather.3.cloned.1.call-done = bf16[2048,2048]{1,0:T(8,128)(2,1)} async-done(((bf16[256,2048]{1,0:T(8,128)(2,1)}), bf16[2048,2048]{1,0:T(8,128)(2,1)}) %all-gather.3.cloned.1.call-update) | async-done | bytes 8388624 | tf_op jit(solution)/shard_map/all_gather | solution.py:149
  58.7 56.0 %gather_fusion = bf16[1024,2048]{1,0:T(8,128)(2,1)} fusion(bf16[8,256,2048]{2,1,0:T(8,128)(2,1)} %bitcast.121, s32[1024]{0:T(1024)S(1)} %get-tuple-element.271), kind=kCustom, calls=%fused_computation | custom fusion | bytes 8396800 | tf_op jit(solution)/shard_map/gather | solution.py:158
  114.7 47.6 %gather_fusion.1 = bf16[1024,2048]{1,0:T(8,128)(2,1)} fusion(bf16[8,256,2048]{2,1,0:T(8,128)(2,1)} %bitcast.122, s32[1024]{0:T(1024)S(1)} %get-tuple-element.271), kind=kCustom, calls=%fused_computation.1 | custom fusion | bytes 8396800 | tf_op jit(solution)/shard_map/gather | solution.py:157
  162.3 4.7 fusion.49
  167.0 2.3 fusion.53
  171.7 3.0 multiply_convert_fusion.10
  174.7 5.6 %fusion.47 = f32[1024,2048]{1,0:T(8,128)} fusion(bf16[1024,512]{1,0:T(8,128)(2,1)S(1)} %get-tuple-element.270, bf16[1,2048,512]{2,1,0:T(8,128)(2,1)S(1)} %copy-done), kind=kOutput, calls=%fused_computation.53 | convolution fusion | flops 2147483648 | bytes 11534336 | tf_op jit(solution)/shard_map/dot_general | solution.py:36
  180.4 5.6 %fusion.51 = f32[1024,2048]{1,0:T(8,128)} fusion(bf16[1024,512]{1,0:T(8,128)(2,1)S(1)} %get-tuple-element.269, bf16[1,2048,512]{2,1,0:T(8,128)(2,1)S(1)} %copy-done.16), kind=kOutput, calls=%fused_computation.57 | convolution fusion | flops 2147483648 | bytes 11534336 | tf_op jit(solution)/shard_map/dot_general | solution.py:39
  186.0 23.7 %scatter_custom_fusion = f32[2048,2048]{1,0:T(8,128)} fusion(s32[1024]{0:T(1024)S(1)} %select_bitcast_fusion, f32[]{:T(128)} %constant.75.clone.1, f32[1024,2048]{1,0:T(8,128)} %fusion.47, f32[1024,2048]{1,0:T(8,128)} %fusion.51), kind=kCustom, calls=%fused_computation.36 | custom fusion | flops 8388608 | bytes 33554436
  209.7 9.1 %convert_element_type.213 = bf16[2048,2048]{1,0:T(8,128)(2,1)} convert(f32[2048,2048]{1,0:T(8,128)} %scatter_custom_fusion) | non-fusion elementwise | flops 4194304 | bytes 25165824 | tf_op jit(solution)/shard_map/convert_element_type | solution.py:168
  221.3 9.2 %all-to-all-start.1 = ((bf16[256,8,256]{0,2,1:T(8,128)(2,1)}), bf16[256,8,256]{0,2,1:T(8,128)(2,1)S(1)}, u32[]{:S(2)}, u32[]{:S(2)}) async-start(bf16[256,8,256]{0,2,1:T(8,128)(2,1)} %bitcast.14), calls=%async_computation.2 | async-start | bytes 2097152 | tf_op jit(solution)/shard_map/all_to_all | solution.py:135
  231.8 14.8 %all-to-all-done.1 = bf16[256,8,256]{0,2,1:T(8,128)(2,1)S(1)} async-done(((bf16[256,8,256]{0,2,1:T(8,128)(2,1)}), bf16[256,8,256]{0,2,1:T(8,128)(2,1)S(1)}, u32[]{:S(2)}, u32[]{:S(2)}) %all-to-all-start.1) | async-done | bytes 1048608 | tf_op jit(solution)/shard_map/all_to_all | solution.py:135
  246.6 3.6 all-to-all-start.3
  250.2 2.3 copy.108
  252.4 15.0 %all-to-all-done.3 = bf16[256,8,256]{0,2,1:T(8,128)(2,1)S(1)} async-done(((bf16[256,8,256]{0,2,1:T(8,128)(2,1)}), bf16[256,8,256]{0,2,1:T(8,128)(2,1)S(1)}, u32[]{:S(2)}, u32[]{:S(2)}) %all-to-all-start.3) | async-done | bytes 1048608 | tf_op jit(solution)/shard_map/all_to_all | solution.py:136
  268.4 4.5 all-to-all-start
  274.4 2.4 reshape.176
  276.9 2.3 copy.117
  283.6 6.6 %all-to-all-done = bf16[256,8,256]{0,2,1:T(8,128)(2,1)} async-done(((bf16[256,8,256]{0,2,1:T(8,128)(2,1)}), bf16[256,8,256]{0,2,1:T(8,128)(2,1)}, u32[]{:S(2)}, u32[]{:S(2)}) %all-to-all-start) | async-done | bytes 1048608 | tf_op jit(solution)/shard_map/all_to_all | solution.py:134
  290.2 2.8 copy.109
  294.6 6.2 %convolution_convert_fusion = bf16[2048,512]{1,0:T(8,128)(2,1)} fusion(bf16[1024,2048]{1,0:T(8,128)(2,1)} %gather_fusion.1, bf16[1024,512]{1,0:T(8,128)(2,1)} %copy-done.18), kind=kOutput, calls=%fused_computation.47 | convolution fusion | flops 2148532224 | bytes 7340032 | tf_op jit(solution)/shard_map/dot_general | solution.py:46
  300.8 2.9 add_convert_fusion.2
  303.7 2.3 copy.131
  305.9 4.2 all-to-all-start.2
  310.3 6.3 %convolution_convert_fusion.1 = bf16[2048,512]{1,0:T(8,128)(2,1)} fusion(bf16[1024,2048]{1,0:T(8,128)(2,1)} %gather_fusion.1, bf16[1024,512]{1,0:T(8,128)(2,1)} %copy-done.17), kind=kOutput, calls=%fused_computation.48 | convolution fusion | flops 2148532224 | bytes 7340032 | tf_op jit(solution)/shard_map/dot_general | solution.py:43
  316.6 4.3 fusion.43
  321.0 6.6 %all-to-all-done.2 = bf16[256,8,256]{0,2,1:T(8,128)(2,1)} async-done(((bf16[256,8,256]{0,2,1:T(8,128)(2,1)}), bf16[256,8,256]{0,2,1:T(8,128)(2,1)}, u32[]{:S(2)}, u32[]{:S(2)}) %all-to-all-start.2) | async-done | bytes 1048608 | tf_op jit(solution)/shard_map/all_to_all | solution.py:183
  327.6 2.8 copy.113
  330.3 2.8 reshape.177
  334.2 117.1 %while.18 = (s32[]{:T(128)}, bf16[2048,2,128]{0,2,1:T(8,128)(2,1)}, f32[2048,2,128]{0,2,1:T(8,128)S(1)}, f32[2048,2,128]{0,2,1:T(8,128)}, bf16[2048,2,128]{0,2,1...) while((s32[]{:T(128)}, bf16[2048,2,128]{0,2,1:T(8,128)(2,1)}, ...), condition=%wide.region_11.12_spmd.clone, body=%wide.region_7.11_spmd.clone.sunk | while | flops 2712404992 | bytes 131359088 | solution.py:107
  334.2 7.5 %fusion.104 = (f32[2,512]{1,0:T(2,128)S(1)}, f32[2,512,2048]{2,1,0:T(8,128)}) fusion(bf16[2048,2,128]{2,0,1:T(8,128)(2,1)} %get-tuple-element.361, bf16[2048,2,128]{0,2,1:T(8,128)(2,1)S(1)} %get-tuple-element.360, s32[]{:T(128)S(6)} %select_n.52), kind=kOutput, calls=%fused_computation.88.clone.1 | convolution fusion | flops 543164416 | bytes 9703428 | tf_op jit(solution)/shard_map/while/body/eval_jaxpr/sub | solution.py:79
  341.7 6.1 %multiply_reduce_fusion.4 = (f32[2,512]{1,0:T(2,128)S(1)}, f32[2,512,2048]{2,1,0:T(8,128)S(1)}) fusion(f32[2,512,2048]{2,1,0:T(8,128)} %get-tuple-element.328, f32[2,512]{1,0:T(2,128)S(1)} %get-tuple-element.329, bf16[2048,2,128]{2,0,1:T(8,128)(2,1)} %get-tuple-element.363, bf16[2048,2,128]{0,2,1:T(8,128)(2,1)} %get-tuple-element.362, s32[]{:T(128)S(6)} %select_n.52), kind=kOutput, calls=%fused_computation.5.clone.1 | convolution fusion | flops 543161344 | bytes 18096132 | tf_op jit(solution)/shard_map/while/body/eval_jaxpr/qhd,khd->hqk/dot_general | solution.py:85
  348.3 2.7 multiply_convert_fusion.14
  351.0 3.4 fusion.106
  356.9 6.0 %fusion.107 = f32[2048,2,128]{0,2,1:T(8,128)} fusion(f32[2048,2,128]{0,2,1:T(8,128)} %get-tuple-element.347, pred[]{:T(512)S(6)} %compare.7, bf16[2048,2,128]{0,2,1:T(8,128)(2,1)} %get-tuple-element.362, s32[]{:T(128)S(6)} %select_n.52, f32[2,512,2048]{2,1,0:T(8,128)} %get-tuple-element.328, f32[2,512]{1,0:T(2,128)S(1)} %get-tuple-element.329), kind=kOutput, calls=%fused_computation.17.clone.1 | convolution fusion | flops 542113792 | bytes 12849157 | tf_op jit(solution)/shard_map/while/body/eval_jaxpr/hqk,qhd->khd/dot_general | solution.py:82
  362.9 7.5 %fusion.104 = (f32[2,512]{1,0:T(2,128)S(1)}, f32[2,512,2048]{2,1,0:T(8,128)}) fusion(bf16[2048,2,128]{2,0,1:T(8,128)(2,1)} %get-tuple-element.361, bf16[2048,2,128]{0,2,1:T(8,128)(2,1)S(1)} %get-tuple-element.360, s32[]{:T(128)S(6)} %select_n.52), kind=kOutput, calls=%fused_computation.88.clone.1 | convolution fusion | flops 543164416 | bytes 9703428 | tf_op jit(solution)/shard_map/while/body/eval_jaxpr/sub | solution.py:79
  370.4 5.9 %multiply_reduce_fusion.4 = (f32[2,512]{1,0:T(2,128)S(1)}, f32[2,512,2048]{2,1,0:T(8,128)S(1)}) fusion(f32[2,512,2048]{2,1,0:T(8,128)} %get-tuple-element.328, f32[2,512]{1,0:T(2,128)S(1)} %get-tuple-element.329, bf16[2048,2,128]{2,0,1:T(8,128)(2,1)} %get-tuple-element.363, bf16[2048,2,128]{0,2,1:T(8,128)(2,1)} %get-tuple-element.362, s32[]{:T(128)S(6)} %select_n.52), kind=kOutput, calls=%fused_computation.5.clone.1 | convolution fusion | flops 543161344 | bytes 18096132 | tf_op jit(solution)/shard_map/while/body/eval_jaxpr/qhd,khd->hqk/dot_general | solution.py:85
  376.8 2.7 multiply_convert_fusion.14
  379.5 3.4 fusion.106
  385.5 6.4 %fusion.107 = f32[2048,2,128]{0,2,1:T(8,128)} fusion(f32[2048,2,128]{0,2,1:T(8,128)} %get-tuple-element.347, pred[]{:T(512)S(6)} %compare.7, bf16[2048,2,128]{0,2,1:T(8,128)(2,1)} %get-tuple-element.362, s32[]{:T(128)S(6)} %select_n.52, f32[2,512,2048]{2,1,0:T(8,128)} %get-tuple-element.328, f32[2,512]{1,0:T(2,128)S(1)} %get-tuple-element.329), kind=kOutput, calls=%fused_computation.17.clone.1 | convolution fusion | flops 542113792 | bytes 12849157 | tf_op jit(solution)/shard_map/while/body/eval_jaxpr/hqk,qhd->khd/dot_general | solution.py:82
  391.9 7.6 %fusion.104 = (f32[2,512]{1,0:T(2,128)S(1)}, f32[2,512,2048]{2,1,0:T(8,128)}) fusion(bf16[2048,2,128]{2,0,1:T(8,128)(2,1)} %get-tuple-element.361, bf16[2048,2,128]{0,2,1:T(8,128)(2,1)S(1)} %get-tuple-element.360, s32[]{:T(128)S(6)} %select_n.52), kind=kOutput, calls=%fused_computation.88.clone.1 | convolution fusion | flops 543164416 | bytes 9703428 | tf_op jit(solution)/shard_map/while/body/eval_jaxpr/sub | solution.py:79
  399.5 6.0 %multiply_reduce_fusion.4 = (f32[2,512]{1,0:T(2,128)S(1)}, f32[2,512,2048]{2,1,0:T(8,128)S(1)}) fusion(f32[2,512,2048]{2,1,0:T(8,128)} %get-tuple-element.328, f32[2,512]{1,0:T(2,128)S(1)} %get-tuple-element.329, bf16[2048,2,128]{2,0,1:T(8,128)(2,1)} %get-tuple-element.363, bf16[2048,2,128]{0,2,1:T(8,128)(2,1)} %get-tuple-element.362, s32[]{:T(128)S(6)} %select_n.52), kind=kOutput, calls=%fused_computation.5.clone.1 | convolution fusion | flops 543161344 | bytes 18096132 | tf_op jit(solution)/shard_map/while/body/eval_jaxpr/qhd,khd->hqk/dot_general | solution.py:85
  405.9 2.7 multiply_convert_fusion.14
  408.6 3.4 fusion.106
  414.4 7.8 %fusion.107 = f32[2048,2,128]{0,2,1:T(8,128)} fusion(f32[2048,2,128]{0,2,1:T(8,128)} %get-tuple-element.347, pred[]{:T(512)S(6)} %compare.7, bf16[2048,2,128]{0,2,1:T(8,128)(2,1)} %get-tuple-element.362, s32[]{:T(128)S(6)} %select_n.52, f32[2,512,2048]{2,1,0:T(8,128)} %get-tuple-element.328, f32[2,512]{1,0:T(2,128)S(1)} %get-tuple-element.329), kind=kOutput, calls=%fused_computation.17.clone.1 | convolution fusion | flops 542113792 | bytes 12849157 | tf_op jit(solution)/shard_map/while/body/eval_jaxpr/hqk,qhd->khd/dot_general | solution.py:82
  422.2 7.6 %fusion.104 = (f32[2,512]{1,0:T(2,128)S(1)}, f32[2,512,2048]{2,1,0:T(8,128)}) fusion(bf16[2048,2,128]{2,0,1:T(8,128)(2,1)} %get-tuple-element.361, bf16[2048,2,128]{0,2,1:T(8,128)(2,1)S(1)} %get-tuple-element.360, s32[]{:T(128)S(6)} %select_n.52), kind=kOutput, calls=%fused_computation.88.clone.1 | convolution fusion | flops 543164416 | bytes 9703428 | tf_op jit(solution)/shard_map/while/body/eval_jaxpr/sub | solution.py:79
  429.8 6.0 %multiply_reduce_fusion.4 = (f32[2,512]{1,0:T(2,128)S(1)}, f32[2,512,2048]{2,1,0:T(8,128)S(1)}) fusion(f32[2,512,2048]{2,1,0:T(8,128)} %get-tuple-element.328, f32[2,512]{1,0:T(2,128)S(1)} %get-tuple-element.329, bf16[2048,2,128]{2,0,1:T(8,128)(2,1)} %get-tuple-element.363, bf16[2048,2,128]{0,2,1:T(8,128)(2,1)} %get-tuple-element.362, s32[]{:T(128)S(6)} %select_n.52), kind=kOutput, calls=%fused_computation.5.clone.1 | convolution fusion | flops 543161344 | bytes 18096132 | tf_op jit(solution)/shard_map/while/body/eval_jaxpr/qhd,khd->hqk/dot_general | solution.py:85
  436.3 2.7 multiply_convert_fusion.14
  439.1 3.4 fusion.106
  444.9 6.4 %fusion.107 = f32[2048,2,128]{0,2,1:T(8,128)} fusion(f32[2048,2,128]{0,2,1:T(8,128)} %get-tuple-element.347, pred[]{:T(512)S(6)} %compare.7, bf16[2048,2,128]{0,2,1:T(8,128)(2,1)} %get-tuple-element.362, s32[]{:T(128)S(6)} %select_n.52, f32[2,512,2048]{2,1,0:T(8,128)} %get-tuple-element.328, f32[2,512]{1,0:T(2,128)S(1)} %get-tuple-element.329), kind=kOutput, calls=%fused_computation.17.clone.1 | convolution fusion | flops 542113792 | bytes 12849157 | tf_op jit(solution)/shard_map/while/body/eval_jaxpr/hqk,qhd->khd/dot_general | solution.py:82
  451.8 1.6 copy.132
  453.4 3.6 all-to-all-start.5
  456.9 1.7 convert_element_type.193
  460.6 13.5 %all-to-all-done.5 = bf16[8,256,256]{2,1,0:T(8,128)(2,1)S(1)} async-done(((bf16[8,256,256]{2,1,0:T(8,128)(2,1)}), bf16[8,256,256]{2,1,0:T(8,128)(2,1)S(1)}, u32[]{:S(2)}, u32[]{:S(2)}) %all-to-all-start.5) | async-done | bytes 1048608 | tf_op jit(solution)/shard_map/all_to_all | solution.py:189
  474.0 3.6 all-to-all-start.6
  480.3 14.5 %all-to-all-done.6 = bf16[8,256,256]{2,1,0:T(8,128)(2,1)S(1)} async-done(((bf16[8,256,256]{2,1,0:T(8,128)(2,1)}), bf16[8,256,256]{2,1,0:T(8,128)(2,1)S(1)}, u32[]{:S(2)}, u32[]{:S(2)}) %all-to-all-start.6) | async-done | bytes 1048608 | tf_op jit(solution)/shard_map/all_to_all | solution.py:190
  494.8 4.5 all-to-all-start.4
  499.4 3.6 fusion.46
  503.0 3.0 fusion.44
  507.3 2.4 copy.127
  511.0 2.3 copy.128
  513.3 3.5 all-to-all-done.4
  516.8 2.3 copy.126
  (151 shorter events, 41.1 us)
Async XLA Ops:
  7.2 155.1 %copy-start = (bf16[1,2048,512]{2,1,0:T(8,128)(2,1)S(1)}, bf16[1,2048,512]{2,1,0:T(8,128)(2,1)}, u32[]{:S(2)}) copy-start(bf16[1,2048,512]{2,1,0:T(8,128)(2,1)} %param.19) | copy-start | bytes 6291460
  7.2 51.5 %all-gather.3.cloned.1.call-start = ((), (), s32[]{:S(2)}) async-start(), calls=%async_computation.8 | async-start | bytes 9437184 | tf_op jit(solution)/shard_map/all_gather | solution.py:149
  7.9 106.8 %all-gather.5.cloned.1.call-start = ((), (), s32[]{:S(2)}) async-start(), calls=%async_computation.9 | async-start | bytes 9437184 | tf_op jit(solution)/shard_map/all_gather | solution.py:148
  8.7 292.1 %reduce-scatter.2.cloned.1.call-start = ((), (), s32[]{:S(2)}) async-start(), calls=%async_computation.10 | async-start | bytes 9437184 | tf_op jit(solution)/shard_map/reduce_scatter | solution.py:167
  162.3 4.7 copy-start.7
  162.3 4.7 copy-start.16
  167.0 3.7 copy-start.19
  167.0 2.9 copy-start.3
  169.4 1.4 copy-start.21
  170.0 1.7 copy-start.15
  174.7 5.7 %copy-start.17 = (bf16[1024,512]{1,0:T(8,128)(2,1)}, bf16[1024,512]{1,0:T(8,128)(2,1)S(1)}, u32[]{:S(2)}) copy-start(bf16[1024,512]{1,0:T(8,128)(2,1)S(1)} %get-tuple-element.270) | copy-start | bytes 3145732
  174.7 5.6 %copy-start.18 = (bf16[1024,512]{1,0:T(8,128)(2,1)}, bf16[1024,512]{1,0:T(8,128)(2,1)S(1)}, u32[]{:S(2)}) copy-start(bf16[1024,512]{1,0:T(8,128)(2,1)S(1)} %get-tuple-element.269) | copy-start | bytes 3145732
  218.8 1.2 copy-start.12
  220.0 10.5 %copy-start.13 = (bf16[256,2048]{1,0:T(8,128)(2,1)S(1)}, bf16[256,2048]{1,0:T(8,128)(2,1)}, u32[]{:S(2)}) copy-start(bf16[256,2048]{1,0:T(8,128)(2,1)} %param.14) | copy-start | bytes 3145732
  221.3 25.2 %all-to-all-start.1 = ((bf16[256,8,256]{0,2,1:T(8,128)(2,1)}), bf16[256,8,256]{0,2,1:T(8,128)(2,1)S(1)}, u32[]{:S(2)}, u32[]{:S(2)}) async-start(bf16[256,8,256]{0,2,1:T(8,128)(2,1)} %bitcast.14), calls=%async_computation.2 | async-start | bytes 2097152 | tf_op jit(solution)/shard_map/all_to_all | solution.py:135
  246.6 20.8 %all-to-all-start.3 = ((bf16[256,8,256]{0,2,1:T(8,128)(2,1)}), bf16[256,8,256]{0,2,1:T(8,128)(2,1)S(1)}, u32[]{:S(2)}, u32[]{:S(2)}) async-start(bf16[256,8,256]{0,2,1:T(8,128)(2,1)} %bitcast.18), calls=%async_computation.4 | async-start | bytes 2097152 | tf_op jit(solution)/shard_map/all_to_all | solution.py:136
  267.4 1.0 copy-start.8
  268.4 21.9 %all-to-all-start = ((bf16[256,8,256]{0,2,1:T(8,128)(2,1)}), bf16[256,8,256]{0,2,1:T(8,128)(2,1)}, u32[]{:S(2)}, u32[]{:S(2)}) async-start(bf16[256,8,256]{0,2,1:T(8,128)(2,1)} %bitcast.12), calls=%async_computation.1 | async-start | bytes 2097152 | tf_op jit(solution)/shard_map/all_to_all | solution.py:134
  274.4 4.7 copy-start.9
  305.9 21.6 %all-to-all-start.2 = ((bf16[256,8,256]{0,2,1:T(8,128)(2,1)}), bf16[256,8,256]{0,2,1:T(8,128)(2,1)}, u32[]{:S(2)}, u32[]{:S(2)}) async-start(bf16[256,8,256]{0,2,1:T(8,128)(2,1)} %bitcast.127), calls=%async_computation.3 | async-start | bytes 2097152 | tf_op jit(solution)/shard_map/all_to_all | solution.py:183
  310.2 189.2 %all-reduce.3.cloned.1.call-start = ((), (), s32[]{:S(2)}) async-start(), calls=%async_computation.11 | async-start | bytes 12582912 | tf_op jit(solution)/shard_map/psum | solution.py:175
  310.2 6.4 %copy-start.4 = (bf16[1024,2048]{1,0:T(8,128)(2,1)S(1)}, bf16[1024,2048]{1,0:T(8,128)(2,1)}, u32[]{:S(2)}) copy-start(bf16[1024,2048]{1,0:T(8,128)(2,1)} %gather_fusion) | copy-start | bytes 12582916
  310.2 6.4 %copy-start.20 = (f32[1024,512]{1,0:T(8,128)S(1)}, f32[1024,512]{1,0:T(8,128)}, u32[]{:S(2)}) copy-start(f32[1024,512]{1,0:T(8,128)} %copy-done.19) | copy-start | bytes 6291460
  310.2 6.4 %copy-start.22 = (f32[1024,512]{1,0:T(8,128)S(1)}, f32[1024,512]{1,0:T(8,128)}, u32[]{:S(2)}) copy-start(f32[1024,512]{1,0:T(8,128)} %copy-done.21) | copy-start | bytes 6291460
  334.2 16.9 %copy-start.5 = (bf16[2048,2,128]{0,2,1:T(8,128)(2,1)}, bf16[2048,2,128]{0,2,1:T(8,128)(2,1)S(1)}, u32[]{:S(2)}) copy-start(bf16[2048,2,128]{0,2,1:T(8,128)(2,1)S(1)} %get-tuple-element.360) | copy-start | bytes 3145732 | tf_op jit(solution)/shard_map/while
  341.7 6.1 %slice-start = ((s8[8388608]{0:T(1024)(128)(4,1)}), s8[4194304]{0:T(1024)(128)(4,1)S(1)}, s32[]{:S(2)}) async-start(s8[8388608]{0:T(1024)(128)(4,1)} %bitcast.119), calls=%async_computation.12 | async-start | bytes 8388608 | tf_op jit(solution)/shard_map/while
  341.7 6.6 %slice-start.1 = ((s8[8388608]{0:T(1024)(128)(4,1)}), s8[4194304]{0:T(1024)(128)(4,1)S(1)}, s32[]{:S(2)}) async-start(s8[8388608]{0:T(1024)(128)(4,1)} %bitcast.119), calls=%async_computation.13 | async-start | bytes 8388608 | tf_op jit(solution)/shard_map/while
  351.0 3.5 copy-start.2
  351.0 3.8 copy-start.14
  356.9 6.0 %copy-start.6 = (bf16[2048,2,128]{0,2,1:T(8,128)(2,1)S(1)}, bf16[2048,2,128]{0,2,1:T(8,128)(2,1)}, u32[]{:S(2)}) copy-start(bf16[2048,2,128]{0,2,1:T(8,128)(2,1)} %copy-done.5) | copy-start | bytes 3145732 | tf_op jit(solution)/shard_map/while
  362.9 16.6 %copy-start.5 = (bf16[2048,2,128]{0,2,1:T(8,128)(2,1)}, bf16[2048,2,128]{0,2,1:T(8,128)(2,1)S(1)}, u32[]{:S(2)}) copy-start(bf16[2048,2,128]{0,2,1:T(8,128)(2,1)S(1)} %get-tuple-element.360) | copy-start | bytes 3145732 | tf_op jit(solution)/shard_map/while
  370.4 5.9 %slice-start = ((s8[8388608]{0:T(1024)(128)(4,1)}), s8[4194304]{0:T(1024)(128)(4,1)S(1)}, s32[]{:S(2)}) async-start(s8[8388608]{0:T(1024)(128)(4,1)} %bitcast.119), calls=%async_computation.12 | async-start | bytes 8388608 | tf_op jit(solution)/shard_map/while
  370.4 6.4 %slice-start.1 = ((s8[8388608]{0:T(1024)(128)(4,1)}), s8[4194304]{0:T(1024)(128)(4,1)S(1)}, s32[]{:S(2)}) async-start(s8[8388608]{0:T(1024)(128)(4,1)} %bitcast.119), calls=%async_computation.13 | async-start | bytes 8388608 | tf_op jit(solution)/shard_map/while
  379.5 3.5 copy-start.2
  379.5 3.8 copy-start.14
  385.5 6.4 %copy-start.6 = (bf16[2048,2,128]{0,2,1:T(8,128)(2,1)S(1)}, bf16[2048,2,128]{0,2,1:T(8,128)(2,1)}, u32[]{:S(2)}) copy-start(bf16[2048,2,128]{0,2,1:T(8,128)(2,1)} %copy-done.5) | copy-start | bytes 3145732 | tf_op jit(solution)/shard_map/while
  391.9 16.6 %copy-start.5 = (bf16[2048,2,128]{0,2,1:T(8,128)(2,1)}, bf16[2048,2,128]{0,2,1:T(8,128)(2,1)S(1)}, u32[]{:S(2)}) copy-start(bf16[2048,2,128]{0,2,1:T(8,128)(2,1)S(1)} %get-tuple-element.360) | copy-start | bytes 3145732 | tf_op jit(solution)/shard_map/while
  399.5 6.0 %slice-start = ((s8[8388608]{0:T(1024)(128)(4,1)}), s8[4194304]{0:T(1024)(128)(4,1)S(1)}, s32[]{:S(2)}) async-start(s8[8388608]{0:T(1024)(128)(4,1)} %bitcast.119), calls=%async_computation.12 | async-start | bytes 8388608 | tf_op jit(solution)/shard_map/while
  399.5 6.4 %slice-start.1 = ((s8[8388608]{0:T(1024)(128)(4,1)}), s8[4194304]{0:T(1024)(128)(4,1)S(1)}, s32[]{:S(2)}) async-start(s8[8388608]{0:T(1024)(128)(4,1)} %bitcast.119), calls=%async_computation.13 | async-start | bytes 8388608 | tf_op jit(solution)/shard_map/while
  408.6 3.5 copy-start.2
  408.6 3.7 copy-start.14
  414.4 7.8 %copy-start.6 = (bf16[2048,2,128]{0,2,1:T(8,128)(2,1)S(1)}, bf16[2048,2,128]{0,2,1:T(8,128)(2,1)}, u32[]{:S(2)}) copy-start(bf16[2048,2,128]{0,2,1:T(8,128)(2,1)} %copy-done.5) | copy-start | bytes 3145732 | tf_op jit(solution)/shard_map/while
  422.2 16.8 %copy-start.5 = (bf16[2048,2,128]{0,2,1:T(8,128)(2,1)}, bf16[2048,2,128]{0,2,1:T(8,128)(2,1)S(1)}, u32[]{:S(2)}) copy-start(bf16[2048,2,128]{0,2,1:T(8,128)(2,1)S(1)} %get-tuple-element.360) | copy-start | bytes 3145732 | tf_op jit(solution)/shard_map/while
  429.8 6.0 %slice-start = ((s8[8388608]{0:T(1024)(128)(4,1)}), s8[4194304]{0:T(1024)(128)(4,1)S(1)}, s32[]{:S(2)}) async-start(s8[8388608]{0:T(1024)(128)(4,1)} %bitcast.119), calls=%async_computation.12 | async-start | bytes 8388608 | tf_op jit(solution)/shard_map/while
  429.8 6.6 %slice-start.1 = ((s8[8388608]{0:T(1024)(128)(4,1)}), s8[4194304]{0:T(1024)(128)(4,1)S(1)}, s32[]{:S(2)}) async-start(s8[8388608]{0:T(1024)(128)(4,1)} %bitcast.119), calls=%async_computation.13 | async-start | bytes 8388608 | tf_op jit(solution)/shard_map/while
  439.0 3.5 copy-start.2
  439.1 3.7 copy-start.14
  444.9 6.4 %copy-start.6 = (bf16[2048,2,128]{0,2,1:T(8,128)(2,1)S(1)}, bf16[2048,2,128]{0,2,1:T(8,128)(2,1)}, u32[]{:S(2)}) copy-start(bf16[2048,2,128]{0,2,1:T(8,128)(2,1)} %copy-done.5) | copy-start | bytes 3145732 | tf_op jit(solution)/shard_map/while
  453.4 20.7 %all-to-all-start.5 = ((bf16[8,256,256]{2,1,0:T(8,128)(2,1)}), bf16[8,256,256]{2,1,0:T(8,128)(2,1)S(1)}, u32[]{:S(2)}, u32[]{:S(2)}) async-start(bf16[8,256,256]{2,1,0:T(8,128)(2,1)} %copy.132), calls=%async_computation.6 | async-start | bytes 2097152 | tf_op jit(solution)/shard_map/all_to_all | solution.py:189
  474.0 20.8 %all-to-all-start.6 = ((bf16[8,256,256]{2,1,0:T(8,128)(2,1)}), bf16[8,256,256]{2,1,0:T(8,128)(2,1)S(1)}, u32[]{:S(2)}, u32[]{:S(2)}) async-start(bf16[8,256,256]{2,1,0:T(8,128)(2,1)} %copy.133), calls=%async_computation.7 | async-start | bytes 2097152 | tf_op jit(solution)/shard_map/all_to_all | solution.py:190
  494.8 21.9 %all-to-all-start.4 = ((bf16[8,256,256]{1,2,0:T(8,128)(2,1)}), bf16[8,256,256]{1,2,0:T(8,128)(2,1)}, u32[]{:S(2)}, u32[]{:S(2)}) async-start(bf16[8,256,256]{1,2,0:T(8,128)(2,1)} %copy.121), calls=%async_computation.5 | async-start | bytes 2097152 | tf_op jit(solution)/shard_map/all_to_all | solution.py:188
  499.4 3.6 copy-start.10
  499.4 3.6 copy-start.11
  507.3 11.8 %copy-start.1 = (bf16[1,2048,512]{2,1,0:T(8,128)(2,1)S(1)}, bf16[1,2048,512]{2,1,0:T(8,128)(2,1)}, u32[]{:S(2)}) copy-start(bf16[1,2048,512]{2,1,0:T(8,128)(2,1)} %param.19) | copy-start | bytes 6291460
Sparse Core Ops, SparseCore 0:
  9.7 48.9 all-gather.2
  60.4 49.9 all-gather.4
  219.0 59.9 reduce-scatter.1
  321.1 124.2 all-reduce.2
where the time goes:
time: 533 us; the launch traced here: 526 us
  local copies, waits for them, and re-layouts  159 us (30%)
  matrix products  138 us (26%)
  waiting for transfers between devices  109 us (20%)
  other arithmetic  59.9 us (11%)
  starting transfers between devices  33.3 us (6%)
  between operations  14.7 us (3%)
  blocking collectives  12.8 us (2%)
    gather x1, local copies, waits for them, and re-layouts, shards(): all_grad.reshape(experts_n, tok_rows, width)[sources, row_index]  56 us
    gather x1, local copies, waits for them, and re-layouts, shards(): all_input.reshape(experts_n, tok_rows, width)[sources, row_index]  47.6 us
    all_gather x1, waiting for transfers between devices, shards(): lax.all_gather(cotangent, 'expert', axis=0, tiled=True)  32.8 us
    sub x4, matrix products, step_block(): expo_scores = jnp.exp(scores - row_max)  30.1 us
    dot_general x4, matrix products, step_block(): jnp.einsum('hqk,qhd->khd', probs_b, grad_blk, preferred_element_type=jnp....  26.5 us
    unnamed x6, other arithmetic  25.2 us
    dot_general x4, matrix products, step_block(): jnp.einsum('qhd,khd->hqk', grad_blk, value_all, preferred_element_type=jn...  24.1 us
    unnamed x49, local copies, waits for them, and re-layouts  21.4 us
  transfers between devices with their start and end apart: 11, of which 8 were waited for; matrix products, arithmetic and copies ran while one was open for 46% of the time, Pallas kernels for 0%

commit v1 on v0

v1 whole, which is shorter than its diff:
```python
import functools
import math

import jax
import jax.numpy as jnp
from jax import lax
from jax.experimental import pallas as pl
from jax.experimental.pallas import tpu as pltpu
from jax.sharding import PartitionSpec as P

TOP = 2

HD = 128
KC = 256
NT = (((1,), (1,)), ((), ()))


def dot(a, b):
    return jnp.dot(a, b, preferred_element_type=jnp.float32)


def dot_nt(a, b):
    return lax.dot_general(a, b, NT, preferred_element_type=jnp.float32)


def attn_kernel(q_ref, do_ref, k_ref, v_ref, dq_ref, dk_ref, dv_ref, s_ref, dp_ref, e_ref, kt_ref, dk_acc, dv_acc):
    step = pl.program_id(1)
    steps = pl.num_programs(1)
    n = k_ref.shape[0]
    chunks = n // KC
    bq = q_ref.shape[0]
    scale = HD ** -0.5
    to_exp2 = scale * math.log2(math.e)

    @pl.when(step == 0)
    def _():
        dk_acc[...] = jnp.zeros_like(dk_acc)
        dv_acc[...] = jnp.zeros_like(dv_acc)
        kt_ref[...] = k_ref[...].T

    q = q_ref[...]
    do = do_ref[...]
    m = None
    for i in range(chunks):
        rows = pl.ds(i * KC, KC)
        s = dot_nt(k_ref[rows, :], q)
        s_ref[rows, :] = s
        top = jnp.max(s, axis=0, keepdims=True)
        m = top if m is None else jnp.maximum(m, top)
        dp_ref[rows, :] = dot_nt(v_ref[rows, :], do)
    total = jnp.zeros((1, bq), jnp.float32)
    delta = jnp.zeros((1, bq), jnp.float32)
    for i in range(chunks):
        rows = pl.ds(i * KC, KC)
        e = jnp.exp2((s_ref[rows, :] - m) * to_exp2)
        total += jnp.sum(e, axis=0, keepdims=True)
        delta += jnp.sum(e * dp_ref[rows, :], axis=0, keepdims=True)
        e_ref[rows, :] = e.astype(jnp.bfloat16)
    inv = 1.0 / total
    delta = delta * inv
    do_t = (do.astype(jnp.float32).T * inv).astype(jnp.bfloat16)
    q_t = (q.astype(jnp.float32).T * inv).astype(jnp.bfloat16)
    dq_t = jnp.zeros((HD, bq), jnp.float32)
    for i in range(chunks):
        rows = pl.ds(i * KC, KC)
        e = e_ref[rows, :]
        dv_acc[rows, :] += dot_nt(e, do_t)
        g = (e.astype(jnp.float32) * (dp_ref[rows, :] - delta)).astype(jnp.bfloat16)
        dk_acc[rows, :] += dot_nt(g, q_t)
        dq_t += dot(kt_ref[:, rows], g)
    dq_ref[...] = (dq_t * (inv * scale)).T.astype(jnp.bfloat16)

    @pl.when(step == steps - 1)
    def _():
        dk_ref[...] = (dk_acc[...] * scale).astype(jnp.bfloat16)
        dv_ref[...] = dv_acc[...].astype(jnp.bfloat16)


def attention(q, k, v, do, bq=512):
    n, width = q.shape
    heads = width // HD
    tile = pl.BlockSpec((bq, HD), lambda h, i: (i, h))
    whole = pl.BlockSpec((n, HD), lambda h, i: (0, h))
    out = jax.ShapeDtypeStruct((n, width), jnp.bfloat16)
    return pl.pallas_call(
        attn_kernel,
        grid=(heads, n // bq),
        in_specs=[tile, tile, whole, whole],
        out_specs=[tile, whole, whole],
        out_shape=[out, out, out],
        scratch_shapes=[
            pltpu.VMEM((n, bq), jnp.float32),
            pltpu.VMEM((n, bq), jnp.float32),
            pltpu.VMEM((n, bq), jnp.bfloat16),
            pltpu.VMEM((HD, n), jnp.bfloat16),
            pltpu.VMEM((n, HD), jnp.float32),
            pltpu.VMEM((n, HD), jnp.float32),
        ],
        compiler_params=pltpu.CompilerParams(vmem_limit_bytes=48 << 20),
        cost_estimate=pl.CostEstimate(flops=10 * n * n * width, bytes_accessed=14 * n * width, transcendentals=heads * n * n),
        name="attention",
    )(q, do, k, v)

MESH = pl.DeviceIdType.MESH
ANY = pl.BlockSpec(memory_space=pl.ANY)


def enter(targets):
    barrier = pltpu.get_barrier_semaphore()
    for target in targets:
        pl.semaphore_signal(barrier, inc=1, device_id=target, device_id_type=MESH)
    pl.semaphore_wait(barrier, len(targets))


def remote(src, dst, send_sem, recv_sem, target):
    return pltpu.make_async_remote_copy(
        src_ref=src,
        dst_ref=dst,
        send_sem=send_sem,
        recv_sem=recv_sem,
        device_id=target,
        device_id_type=MESH,
    )


def strip(index, size):
    return pl.ds(pl.multiple_of(index * size, size), size)


def start_to_heads(srcs, dsts, send_sem, recv_sem, local_sem):
    me = lax.axis_index("seq")
    copies = []
    for a, (src, dst) in enumerate(zip(srcs, dsts)):
        for d in range(1, 8):
            to = lax.rem(me + d, 8)
            copies.append(
                remote(
                    src.at[:, strip(to, 256)],
                    dst.at[strip(me, 256), :],
                    send_sem.at[a, d],
                    recv_sem.at[a, d],
                    {"seq": to},
                )
            )
            copies[-1].start()
        copies.append(
            pltpu.make_async_copy(
                src.at[:, strip(me, 256)], dst.at[strip(me, 256), :], local_sem.at[a]
            )
        )
        copies[-1].start()
    return copies


def start_to_tokens(srcs, dsts, send_sem, recv_sem, local_sem):
    me = lax.axis_index("seq")
    copies = []
    for a, (src, dst) in enumerate(zip(srcs, dsts)):
        for d in range(1, 8):
            to = lax.rem(me + d, 8)
            copies.append(
                remote(
                    src.at[strip(to, 256), :],
                    dst.at[:, strip(me, 256)],
                    send_sem.at[a, d],
                    recv_sem.at[a, d],
                    {"seq": to},
                )
            )
            copies[-1].start()
        copies.append(
            pltpu.make_async_copy(
                src.at[strip(me, 256), :], dst.at[:, strip(me, 256)], local_sem.at[a]
            )
        )
        copies[-1].start()
    return copies


def seq_peers():
    me = lax.axis_index("seq")
    return [{"seq": lax.rem(me + d, 8)} for d in range(1, 8)]


def swap_kernel(start, count, *refs):
    srcs, dsts, sems = refs[:count], refs[count : 2 * count], refs[2 * count :]
    enter(seq_peers())
    for copy in start(srcs, dsts, *sems):
        copy.wait()


def swap(start, arrays, shape, collective_id, name):
    count = len(arrays)
    return pl.pallas_call(
        functools.partial(swap_kernel, start, count),
        out_shape=[jax.ShapeDtypeStruct(shape, jnp.bfloat16)] * count,
        in_specs=[ANY] * count,
        out_specs=[ANY] * count,
        scratch_shapes=[
            pltpu.SemaphoreType.DMA((count, 8)),
            pltpu.SemaphoreType.DMA((count, 8)),
            pltpu.SemaphoreType.DMA((count,)),
        ],
        compiler_params=pltpu.CompilerParams(collective_id=collective_id, has_side_effects=True),
        name=name,
    )(*arrays)


def sibling(index):
    return index + 1 - 2 * lax.rem(index, 2)


def spread_kernel(
    x_ref, c_ref, t_ref, q_ref, k_ref, v_ref,
    all_x, all_c, all_t, head_q, head_k, head_v,
    send_sem, recv_sem, local_sem, t_send, t_recv, seq_send, seq_recv, seq_local,
):
    me = lax.axis_index("expert")
    right, left, across = [lax.rem(me + d, 8) for d in (2, 6, 4)]
    pair = sibling(me)
    enter([{"expert": lax.rem(me + d, 8)} for d in range(1, 8)] + seq_peers())
    srcs, outs = (x_ref, c_ref), (all_x, all_c)
    sends = []

    def piece(a, half, owner, mine, target, send_at, recv_at):
        rows = pl.ds(half * 128, 128)
        src = srcs[a].at[rows, :] if mine else outs[a].at[owner, rows, :]
        return remote(
            src,
            outs[a].at[owner, rows, :],
            send_sem.at[send_at],
            recv_sem.at[recv_at],
            {"expert": target},
        )

    def recv_index(kind, a, half):
        return kind * 4 + a * 2 + half

    def send(a, half, owner, mine, target, kind):
        copy = piece(a, half, owner, mine, target, len(sends), recv_index(kind, a, half))
        copy.start()
        sends.append(copy)

    def arrived(a, half, owner, kind):
        piece(a, half, owner, False, me, 0, recv_index(kind, a, half)).wait_recv()

    small = []
    for d in range(1, 8):
        to = lax.rem(me + d, 8)
        copy = remote(t_ref, all_t.at[me], t_send.at[d], t_recv.at[d], {"expert": to})
        copy.start()
        small.append(copy)
    for a in (0, 1):
        for half in (0, 1):
            send(a, half, me, True, right, 0)
            send(a, 1 - half, me, True, left, 1)
        for half in (0, 1):
            send(a, half, me, True, pair, 3)
    local = [
        pltpu.make_async_copy(x_ref, all_x.at[me], local_sem.at[0]),
        pltpu.make_async_copy(c_ref, all_c.at[me], local_sem.at[1]),
        pltpu.make_async_copy(t_ref, all_t.at[me], local_sem.at[2]),
    ]
    for copy in local:
        copy.start()
    heads = start_to_heads(
        (q_ref, k_ref, v_ref), (head_q, head_k, head_v), seq_send, seq_recv, seq_local
    )
    for a in (0, 1):
        arrived(a, 0, left, 0)
        send(a, 0, left, False, right, 2)
        send(a, 0, left, False, pair, 4)
        arrived(a, 1, right, 1)
        send(a, 1, right, False, left, 2)
        send(a, 1, right, False, pair, 5)
        arrived(a, 1, left, 0)
        send(a, 1, left, False, pair, 4)
        arrived(a, 0, right, 1)
        send(a, 0, right, False, pair, 5)
    for a in (0, 1):
        for half in (0, 1):
            arrived(a, half, across, 2)
            send(a, half, across, False, pair, 6)
    for a in (0, 1):
        for half in (0, 1):
            for kind, owner in ((3, me), (4, left), (5, right), (6, across)):
                arrived(a, half, sibling(owner), kind)
    for copy in sends:
        copy.wait_send()
    for copy in local + small + heads:
        copy.wait()


def spread(x, c, table, q, k, v):
    shapes = [(8, 256, 2048)] * 2 + [(8, 8, 256)] + [(2048, 256)] * 3
    types = [jnp.bfloat16] * 2 + [jnp.float32] + [jnp.bfloat16] * 3
    dma = pltpu.SemaphoreType.DMA
    return pl.pallas_call(
        spread_kernel,
        out_shape=[jax.ShapeDtypeStruct(s, t) for s, t in zip(shapes, types)],
        in_specs=[ANY] * 6,
        out_specs=[ANY] * 6,
        scratch_shapes=[
            dma((28,)), dma((28,)), dma((3,)), dma((8,)), dma((8,)), dma((3, 8)), dma((3, 8)), dma((3,)),
        ],
        compiler_params=pltpu.CompilerParams(collective_id=1, has_side_effects=True),
        name="spread",
    )(x, c, table, q, k, v)


def expert_backward(rows_in, scaled_grad, gate_matrix, up_matrix, down_matrix):
    first = (((0,), (0,)), ((), ()))
    gate_value = dot(rows_in, gate_matrix)
    up_value = dot(rows_in, up_matrix)
    sigmoid_gate = jax.nn.sigmoid(gate_value)
    activated = gate_value * sigmoid_gate
    inner_value = (activated * up_value).astype(jnp.bfloat16)
    grad_inner = dot_nt(scaled_grad, down_matrix)
    grad_gate_value = (
        grad_inner * up_value * sigmoid_gate * (1.0 + gate_value * (1.0 - sigmoid_gate))
    ).astype(jnp.bfloat16)
    grad_up_value = (grad_inner * activated).astype(jnp.bfloat16)
    hidden_part = dot_nt(grad_gate_value, gate_matrix) + dot_nt(grad_up_value, up_matrix)
    parts = [
        lax.dot_general(a, b, first, preferred_element_type=jnp.float32).astype(jnp.bfloat16)
        for a, b in (
            (rows_in, grad_gate_value),
            (rows_in, grad_up_value),
            (inner_value, scaled_grad),
        )
    ]
    return hidden_part.astype(jnp.bfloat16), parts


def shards(
    attn_query, attn_key, attn_value, moe_input, cotangent,
    routes, route_weight, w_gate, w_up, w_down,
):
    rows, width = moe_input.shape
    experts = lax.axis_size("expert")
    mine = lax.axis_index("expert")
    expert_ids = jnp.arange(experts, dtype=jnp.int32)
    hits = routes.T[:, None, :] == expert_ids[None, :, None]
    table = jnp.sum(
        jnp.where(hits, route_weight.astype(jnp.float32).T[:, None, :], 0.0), axis=0
    )
    all_x, all_c, all_t, head_q, head_k, head_v = spread(
        moe_input, cotangent, table, attn_query, attn_key, attn_value
    )
    own = lax.dynamic_slice_in_dim(all_t, mine, 1, 1)[:, 0]
    taken = own > 0.0
    rank = jnp.cumsum(taken.astype(jnp.int32), axis=1) - 1
    slot_ids = jnp.arange(128, dtype=jnp.int32)
    matched = (rank[:, None, :] == slot_ids[None, :, None]) & taken[:, None, :]
    pick = matched.astype(jnp.bfloat16)
    pick_weight = jnp.where(matched, own[:, None, :], 0.0).astype(jnp.bfloat16)
    rows_in = jnp.einsum("bst,btd->bsd", pick, all_x).reshape(-1, width)
    scaled_grad = jnp.einsum("bst,btd->bsd", pick_weight, all_c).reshape(-1, width)
    hidden_part, parts = expert_backward(rows_in, scaled_grad, w_gate[0], w_up[0], w_down[0])
    terms = jnp.einsum("bst,bsd->btd", pick, hidden_part.reshape(8, 128, width))
    routed_sum = lax.psum_scatter(
        terms.reshape(experts * rows, width), "expert", scatter_dimension=0, tiled=True
    ).astype(jnp.float32)
    grad_hidden = (cotangent.astype(jnp.float32) + routed_sum).astype(jnp.bfloat16)
    sums = [lax.psum(part, ("dp", "seq")).astype(jnp.float32) for part in parts]
    groups = jnp.float32(lax.axis_size("dp") * lax.axis_size("seq"))
    grads = [(total / groups)[None].astype(jnp.bfloat16) for total in sums]
    (head_grad,) = swap(start_to_heads, [grad_hidden], (2048, 256), 2, "grad_to_heads")
    backs = attention(head_q, head_k, head_v, head_grad)
    grad_query, grad_key, grad_value = swap(
        start_to_tokens, backs, (rows, width), 3, "grads_to_tokens"
    )
    return (grad_hidden, grad_query, grad_key, grad_value, *grads)


def solution(mesh):
    tokens = P(("dp", "expert", "seq"), None)
    weights = P("expert", None, None)
    return jax.shard_map(
        shards,
        mesh=mesh,
        in_specs=(tokens,) * 7 + (weights,) * 3,
        out_specs=(tokens,) * 4 + (weights,) * 3,
        check_vma=False,
    )
```

time: 533 us -> 372 us (0.70)
  the two profiles are of different devices: /device:TPU:104 before, /device:TPU:6 now
where the time goes in v1:
time: 372 us
  Pallas kernels  186 us (50%)
  waiting for transfers between devices  111 us (30%)
  matrix products  37.1 us (10%)
  between operations  15.8 us (4%)
  other arithmetic  12.8 us (3%)
  local copies, waits for them, and re-layouts  8.82 us (2%)
    psum x1, waiting for transfers between devices, shards(): sums = [lax.psum(part, ('dp', 'seq')).astype(jnp.float32) for part in parts]  111 us
    pallas_call x1, Pallas kernels, spread(): pl.pallas_call(spread_kernel, out_shape=[jax.ShapeDtypeStruct(s, t) for s...  82 us
    pallas_call x2, Pallas kernels, swap(): pl.pallas_call(functools.partial(swap_kernel, start, count), out_shape=[j...  61.4 us
    pallas_call x1, Pallas kernels, attention(): pl.pallas_call(attn_kernel, grid=(heads, n // bq), in_specs=[tile, tile,...  42.6 us
    dot_general x3, matrix products, expert_backward(): lax.dot_general(a, b, first, preferred_element_type=jnp.float32)  11.5 us
    dot_general x3, matrix products, dot_nt(): return lax.dot_general(a, b, NT, preferred_element_type=jnp.float32)  9.22 us
    unnamed x41, local copies, waits for them, and re-layouts  8.6 us
  transfers between devices with their start and end apart: 2, of which 1 were waited for; matrix products, arithmetic and copies ran while one was open for 5% of the time, Pallas kernels for 0%

profile of v1, /device:TPU:6, one launch (start us, length us, event | category | flops | bytes accessed | tf_op | source)
XLA Modules:
  0.0 372.0 jit_solution(2838007565525853299)
XLA Ops:
  8.0 0.0 copy-start
  8.0 0.0 all-reduce.3.cloned.1.call-start
  8.1 0.8 convert_bitcast_fusion
  8.9 1.3 select_reduce_fusion.t_ref
  10.2 82.0 %spread.1 = (bf16[8,256,2048]{2,1,0:T(8,128)(2,1)}, bf16[8,256,2048]{2,1,0:T(8,128)(2,1)}, f32[8,8,256]{2,1,0:T(8,128)}, bf16[2048,256]{1,0:T(8,128)(2,1)}, bf16...) custom-call(bf16[256,2048]{1,0:T(8,128)(2,1)} %x_ref.1, bf16[256,2048]{1,0:T(8,128)(2,1)} %c_ref.1, ...), custom_call_target="tpu_custom_call" | custom-call | tf_op jit(solution)/shard_map/spread/pallas_call | solution.py:298
  92.1 0.9 broadcast_compare_fusion
  93.1 0.6 reduce-window.6
  93.7 0.2 slice_reduce_fusion
  93.9 0.1 add_bitcast_fusion
  94.0 4.5 %fusion.16 = bf16[8,128,2048]{2,1,0:T(8,128)(2,1)S(1)} fusion(bf16[8,256,2048]{2,1,0:T(8,128)(2,1)} %get-tuple-element.21, s32[8,256]{1,0:T(8,128)S(1)} %add_bitcast_fusion, pred[8,256]{1,0:T(8,128)(4,1)S(1)} %bitcast.60), kind=kOutput, calls=%fused_computation.29 | convolution fusion | flops 1074266112 | bytes 12593152 | tf_op jit(solution)/shard_map/bst,btd->bsd/dot_general | solution.py:357
  98.5 0.0 copy-done
  98.5 0.0 copy-start.13
  98.5 0.0 slice-start
  98.5 2.3 fusion.5
  100.8 0.0 copy-done.13
  100.8 0.0 slice-start.1
  100.9 2.3 fusion.8
  103.2 0.0 slice-done
  103.2 0.0 slice-done.1
  103.2 2.3 fusion.18
  105.5 0.0 copy-start.12
  105.5 4.0 %convolution_convert_fusion = bf16[512,2048]{1,0:T(8,128)(2,1)} fusion(bf16[1024,2048]{1,0:T(8,128)(2,1)S(1)} %bitcast.58, f32[1024,512]{1,0:T(8,128)S(1)} %fusion.8, f32[1024,512]{1,0:T(8,128)S(1)} %fusion.5), kind=kOutput, calls=%fused_computation.4 | convolution fusion | flops 2151677952 | bytes 10485760 | tf_op jit(solution)/shard_map/dot_general | solution.py:325
  109.5 0.0 copy-done.12
  109.5 3.0 multiply_convert_fusion.4
  112.5 0.0 copy-start.15
  112.6 3.8 %convolution_convert_fusion.1 = bf16[2048,512]{1,0:T(8,128)(2,1)} fusion(bf16[1024,2048]{1,0:T(8,128)(2,1)S(1)} %bitcast.56, bf16[1024,512]{1,0:T(8,128)(2,1)S(1)} %get-tuple-element.36), kind=kOutput, calls=%fused_computation.5 | convolution fusion | flops 2148532224 | bytes 7340032 | tf_op jit(solution)/shard_map/dot_general | solution.py:325
  116.3 0.0 copy-done.15
  116.3 3.8 %convolution_convert_fusion.2 = bf16[2048,512]{1,0:T(8,128)(2,1)} fusion(bf16[1024,2048]{1,0:T(8,128)(2,1)S(1)} %bitcast.57, bf16[1024,512]{1,0:T(8,128)(2,1)S(1)} %get-tuple-element.37), kind=kOutput, calls=%fused_computation.6 | convolution fusion | flops 2148532224 | bytes 7340032 | tf_op jit(solution)/shard_map/dot_general | solution.py:325
  120.1 0.0 all-reduce.3.cloned.1.call-update
  120.1 0.3 reduce-scatter.2.cloned.1.call-start
  120.4 0.0 copy-start.14
  120.4 3.7 %fusion.3 = f32[1024,2048]{1,0:T(8,128)S(1)} fusion(bf16[1024,512]{1,0:T(8,128)(2,1)} %copy-done.15, bf16[1,2048,512]{2,1,0:T(8,128)(2,1)S(1)} %copy-done), kind=kOutput, calls=%fused_computation.10 | convolution fusion | flops 2147483648 | bytes 11534336 | tf_op jit(solution)/shard_map/dot_general | solution.py:23
  124.2 0.0 copy-done.14
  124.2 2.4 add_convert_fusion
  126.6 4.9 %fusion.14 = bf16[8,256,2048]{2,1,0:T(8,128)(2,1)} fusion(bf16[8,128,2048]{2,1,0:T(8,128)(2,1)S(1)} %bitcast.53, s32[8,256]{1,0:T(8,128)S(1)} %add_bitcast_fusion, pred[8,256]{1,0:T(8,128)(4,1)S(1)} %bitcast.62), kind=kOutput, calls=%fused_computation.28 | convolution fusion | flops 1074266112 | bytes 12593152 | tf_op jit(solution)/shard_map/bst,bsd->btd/dot_general | solution.py:360
  131.6 0.0 reduce-scatter.2.cloned.1.call-update
  131.6 111.1 %all-reduce.3.cloned.1.call-done = (bf16[2048,512]{1,0:T(8,128)(2,1)}, bf16[2048,512]{1,0:T(8,128)(2,1)}, bf16[512,2048]{1,0:T(8,128)(2,1)}) async-done(((bf16[2048,512]{1,0:T(8,128)(2,1)}, bf16[2048,512]{1,0:T(8,128)(2,1)}, bf16[512,2048]{1,0:T(8,128)(2,1)}), (bf16[2048,512]{1,0:T(8,128)(2,1)}, bf16[2048,512]{1,0:T(8,128)(2,1)}, bf16[512,2048]{1,0:T(8,128)(2,1)})) %all-reduce.3.cloned.1.call-update) | async-done | bytes 6291472 | tf_op jit(solution)/shard_map/psum | solution.py:365
  242.7 0.0 copy-start.8
  242.7 0.0 copy-start.9
  242.7 3.6 fusion.2
  246.3 0.0 copy-done.8
  246.3 0.0 copy-done.9
  246.3 2.9 fusion
  249.2 0.0 copy-done.7
  249.2 2.7 add_convert_fusion.1.refs_0_
  251.9 19.2 %grad_to_heads.1.do_ref = bf16[2048,256]{1,0:T(8,128)(2,1)} custom-call(bf16[256,2048]{1,0:T(8,128)(2,1)} %add_convert_fusion.1.refs_0_), custom_call_target="tpu_custom_call" | custom-call | tf_op jit(solution)/shard_map/grad_to_heads/pallas_call | solution.py:194
  271.0 0.0 copy-done.6
  271.0 0.0 copy-start.5
  271.0 1.2 copy-done.5
  272.3 42.6 %attention.1 = (bf16[2048,256]{1,0:T(8,128)(2,1)S(1)}, bf16[2048,256]{1,0:T(8,128)(2,1)S(1)}, bf16[2048,256]{1,0:T(8,128)(2,1)S(1)}) custom-call(bf16[2048,256]{1,0:T(8,128)(2,1)S(1)} %copy-done.6, bf16[2048,256]{1,0:T(8,128)(2,1)S(1)} %copy-done.5, bf16[2048,256]{1,0:T(8,128)(2,1)} %get-tuple-element.23.k_ref, bf16[2048,256]{1,0:T(8,128)(2,1)} %get-tuple-element.24.v_ref), custom_call_target="tpu_custom_call" | custom-call | flops 10737418240 | bytes 7340032 | tf_op jit(solution)/shard_map/attention/pallas_call | solution.py:85
  314.9 0.0 copy-start.2
  314.9 1.0 copy-done.2
  315.8 1.0 copy-done.3
  316.8 1.0 copy-done.4
  317.8 42.3 %grads_to_tokens.1 = (bf16[256,2048]{1,0:T(8,128)(2,1)}, bf16[256,2048]{1,0:T(8,128)(2,1)}, bf16[256,2048]{1,0:T(8,128)(2,1)}) custom-call(bf16[2048,256]{1,0:T(8,128)(2,1)} %copy-done.2, bf16[2048,256]{1,0:T(8,128)(2,1)} %copy-done.3, bf16[2048,256]{1,0:T(8,128)(2,1)} %copy-done.4), custom_call_target="tpu_custom_call" | custom-call | tf_op jit(solution)/shard_map/grads_to_tokens/pallas_call | solution.py:194
  360.1 0.0 copy-start.11
  360.1 0.0 copy-start.10
  360.1 0.0 copy-start.1
  360.1 2.5 copy.40
  362.6 0.0 copy-done.11
  362.6 1.0 copy.41
  363.5 0.0 copy-done.10
  363.6 1.0 copy.42
  364.5 0.0 copy-done.1
  (12 shorter events, 0.1 us)
Async XLA Ops:
  8.0 90.5 %copy-start = (bf16[1,2048,512]{2,1,0:T(8,128)(2,1)S(1)}, bf16[1,2048,512]{2,1,0:T(8,128)(2,1)}, u32[]{:S(2)}) copy-start(bf16[1,2048,512]{2,1,0:T(8,128)(2,1)} %param.17) | copy-start | bytes 6291460
  8.0 234.7 %all-reduce.3.cloned.1.call-start = ((), (), s32[]{:S(2)}) async-start(), calls=%async_computation.2 | async-start | bytes 12582912 | tf_op jit(solution)/shard_map/psum | solution.py:365
  98.5 2.4 copy-start.13
  98.5 4.7 %slice-start = ((s8[8388608]{0:T(1024)(128)(4,1)}), s8[4194304]{0:T(1024)(128)(4,1)S(1)}, s32[]{:S(2)}) async-start(s8[8388608]{0:T(1024)(128)(4,1)} %bitcast.51), calls=%async_computation.3 | async-start | bytes 8388608
  100.8 2.4 slice-start.1
  105.5 4.0 %copy-start.12 = (bf16[1,512,2048]{2,1,0:T(8,128)(2,1)S(1)}, bf16[1,512,2048]{2,1,0:T(8,128)(2,1)}, u32[]{:S(2)}) copy-start(bf16[1,512,2048]{2,1,0:T(8,128)(2,1)} %param.19) | copy-start | bytes 6291460
  112.5 3.8 %copy-start.15 = (bf16[1024,512]{1,0:T(8,128)(2,1)}, bf16[1024,512]{1,0:T(8,128)(2,1)S(1)}, u32[]{:S(2)}) copy-start(bf16[1024,512]{1,0:T(8,128)(2,1)S(1)} %get-tuple-element.37) | copy-start | bytes 3145732
  120.1 129.1 %reduce-scatter.2.cloned.1.call-start = ((), (), s32[]{:S(2)}) async-start(), calls=%async_computation.1 | async-start | bytes 9437184 | tf_op jit(solution)/shard_map/reduce_scatter | solution.py:361
  120.4 3.8 %copy-start.14 = (bf16[1,2048,512]{2,1,0:T(8,128)(2,1)S(1)}, bf16[1,2048,512]{2,1,0:T(8,128)(2,1)}, u32[]{:S(2)}) copy-start(bf16[1,2048,512]{2,1,0:T(8,128)(2,1)} %param.18) | copy-start | bytes 6291460
  242.7 3.6 copy-start.8
  242.7 3.6 copy-start.9
  246.3 2.9 copy-start.7
  249.2 21.8 %copy-start.6 = (bf16[2048,256]{1,0:T(8,128)(2,1)S(1)}, bf16[2048,256]{1,0:T(8,128)(2,1)}, u32[]{:S(2)}) copy-start(bf16[2048,256]{1,0:T(8,128)(2,1)} %get-tuple-element.22.q_ref) | copy-start | bytes 3145732
  271.0 1.2 copy-start.5
  314.9 1.0 copy-start.2
  315.8 1.0 copy-start.3
  316.8 1.0 copy-start.4
  360.1 2.5 copy-start.11
  360.1 3.5 copy-start.10
  360.1 4.4 %copy-start.1 = (bf16[1,2048,512]{2,1,0:T(8,128)(2,1)S(1)}, bf16[1,2048,512]{2,1,0:T(8,128)(2,1)}, u32[]{:S(2)}) copy-start(bf16[1,2048,512]{2,1,0:T(8,128)(2,1)} %param.17) | copy-start | bytes 6291460
Sparse Core Ops, SparseCore 0:
  120.2 122.4 all-reduce.2
Sparse Core Ops, SparseCore 1:
  131.7 52.7 reduce-scatter.1

commit v2 on v1

--- a/solution.py
+++ b/solution.py
@@ -11,7 +11,6 @@
 TOP = 2
 
 HD = 128
-KC = 256
 NT = (((1,), (1,)), ((), ()))
 
 
@@ -22,84 +21,6 @@
 def dot_nt(a, b):
     return lax.dot_general(a, b, NT, preferred_element_type=jnp.float32)
 
-
-def attn_kernel(q_ref, do_ref, k_ref, v_ref, dq_ref, dk_ref, dv_ref, s_ref, dp_ref, e_ref, kt_ref, dk_acc, dv_acc):
-    step = pl.program_id(1)
-    steps = pl.num_programs(1)
-    n = k_ref.shape[0]
-    chunks = n // KC
-    bq = q_ref.shape[0]
-    scale = HD ** -0.5
-    to_exp2 = scale * math.log2(math.e)
-
-    @pl.when(step == 0)
-    def _():
-        dk_acc[...] = jnp.zeros_like(dk_acc)
-        dv_acc[...] = jnp.zeros_like(dv_acc)
-        kt_ref[...] = k_ref[...].T
-
-    q = q_ref[...]
-    do = do_ref[...]
-    m = None
-    for i in range(chunks):
-        rows = pl.ds(i * KC, KC)
-        s = dot_nt(k_ref[rows, :], q)
-        s_ref[rows, :] = s
-        top = jnp.max(s, axis=0, keepdims=True)
-        m = top if m is None else jnp.maximum(m, top)
-        dp_ref[rows, :] = dot_nt(v_ref[rows, :], do)
-    total = jnp.zeros((1, bq), jnp.float32)
-    delta = jnp.zeros((1, bq), jnp.float32)
-    for i in range(chunks):
-        rows = pl.ds(i * KC, KC)
-        e = jnp.exp2((s_ref[rows, :] - m) * to_exp2)
-        total += jnp.sum(e, axis=0, keepdims=True)
-        delta += jnp.sum(e * dp_ref[rows, :], axis=0, keepdims=True)
-        e_ref[rows, :] = e.astype(jnp.bfloat16)
-    inv = 1.0 / total
-    delta = delta * inv
-    do_t = (do.astype(jnp.float32).T * inv).astype(jnp.bfloat16)
-    q_t = (q.astype(jnp.float32).T * inv).astype(jnp.bfloat16)
-    dq_t = jnp.zeros((HD, bq), jnp.float32)
-    for i in range(chunks):
-        rows = pl.ds(i * KC, KC)
-        e = e_ref[rows, :]
-        dv_acc[rows, :] += dot_nt(e, do_t)
-        g = (e.astype(jnp.float32) * (dp_ref[rows, :] - delta)).astype(jnp.bfloat16)
-        dk_acc[rows, :] += dot_nt(g, q_t)
-        dq_t += dot(kt_ref[:, rows], g)
-    dq_ref[...] = (dq_t * (inv * scale)).T.astype(jnp.bfloat16)
-
-    @pl.when(step == steps - 1)
-    def _():
-        dk_ref[...] = (dk_acc[...] * scale).astype(jnp.bfloat16)
-        dv_ref[...] = dv_acc[...].astype(jnp.bfloat16)
-
-
-def attention(q, k, v, do, bq=512):
-    n, width = q.shape
-    heads = width // HD
-    tile = pl.BlockSpec((bq, HD), lambda h, i: (i, h))
-    whole = pl.BlockSpec((n, HD), lambda h, i: (0, h))
-    out = jax.ShapeDtypeStruct((n, width), jnp.bfloat16)
-    return pl.pallas_call(
-        attn_kernel,
-        grid=(heads, n // bq),
-        in_specs=[tile, tile, whole, whole],
-        out_specs=[tile, whole, whole],
-        out_shape=[out, out, out],
-        scratch_shapes=[
-            pltpu.VMEM((n, bq), jnp.float32),
-            pltpu.VMEM((n, bq), jnp.float32),
-            pltpu.VMEM((n, bq), jnp.bfloat16),
-            pltpu.VMEM((HD, n), jnp.bfloat16),
-            pltpu.VMEM((n, HD), jnp.float32),
-            pltpu.VMEM((n, HD), jnp.float32),
-        ],
-        compiler_params=pltpu.CompilerParams(vmem_limit_bytes=48 << 20),
-        cost_estimate=pl.CostEstimate(flops=10 * n * n * width, bytes_accessed=14 * n * width, transcendentals=heads * n * n),
-        name="attention",
-    )(q, do, k, v)
 
 MESH = pl.DeviceIdType.MESH
 ANY = pl.BlockSpec(memory_space=pl.ANY)
@@ -152,58 +73,9 @@
     return copies
 
 
-def start_to_tokens(srcs, dsts, send_sem, recv_sem, local_sem):
-    me = lax.axis_index("seq")
-    copies = []
-    for a, (src, dst) in enumerate(zip(srcs, dsts)):
-        for d in range(1, 8):
-            to = lax.rem(me + d, 8)
-            copies.append(
-                remote(
-                    src.at[strip(to, 256), :],
-                    dst.at[:, strip(me, 256)],
-                    send_sem.at[a, d],
-                    recv_sem.at[a, d],
-                    {"seq": to},
-                )
-            )
-            copies[-1].start()
-        copies.append(
-            pltpu.make_async_copy(
-                src.at[strip(me, 256), :], dst.at[:, strip(me, 256)], local_sem.at[a]
-            )
-        )
-        copies[-1].start()
-    return copies
-
-
 def seq_peers():
     me = lax.axis_index("seq")
     return [{"seq": lax.rem(me + d, 8)} for d in range(1, 8)]
-
-
-def swap_kernel(start, count, *refs):
-    srcs, dsts, sems = refs[:count], refs[count : 2 * count], refs[2 * count :]
-    enter(seq_peers())
-    for copy in start(srcs, dsts, *sems):
-        copy.wait()
-
-
-def swap(start, arrays, shape, collective_id, name):
-    count = len(arrays)
-    return pl.pallas_call(
-        functools.partial(swap_kernel, start, count),
-        out_shape=[jax.ShapeDtypeStruct(shape, jnp.bfloat16)] * count,
-        in_specs=[ANY] * count,
-        out_specs=[ANY] * count,
-        scratch_shapes=[
-            pltpu.SemaphoreType.DMA((count, 8)),
-            pltpu.SemaphoreType.DMA((count, 8)),
-            pltpu.SemaphoreType.DMA((count,)),
-        ],
-        compiler_params=pltpu.CompilerParams(collective_id=collective_id, has_side_effects=True),
-        name=name,
-    )(*arrays)
 
 
 def sibling(index):
@@ -308,6 +180,379 @@
     )(x, c, table, q, k, v)
 
 
+def add_rows(out, terms, rows, step):
+    @pl.loop(0, rows, step=step)
+    def _(at):
+        at = pl.multiple_of(at, step)
+        total = None
+        for ref, base in terms:
+            value = ref[pl.ds(pl.multiple_of(base + at, step), step), :].astype(jnp.float32)
+            total = value if total is None else total + value
+        ref, base, factor = out
+        if factor is not None:
+            total = total * factor
+        ref[pl.ds(pl.multiple_of(base + at, step), step), :] = total.astype(jnp.bfloat16)
+
+
+def flip(index):
+    return index + 1 - 2 * lax.rem(index, 2)
+
+
+def forward_block(index, q, k, vt, s, e, ot, inv, qt):
+    h = lax.div(index, 8)
+    at = lax.rem(index, 8)
+    cols = strip(at, 256)
+    to_exp2 = (HD ** -0.5) * math.log2(math.e)
+    query = q[h, cols, :]
+    top = None
+    for i in range(8):
+        rows = pl.ds(i * 256, 256)
+        score = dot_nt(k[h, rows, :], query)
+        s[rows, :] = score
+        peak = jnp.max(score, axis=0, keepdims=True)
+        top = peak if top is None else jnp.maximum(top, peak)
+    total = jnp.zeros((1, 256), jnp.float32)
+    attended = jnp.zeros((HD, 256), jnp.float32)
+    for i in range(8):
+        rows = pl.ds(i * 256, 256)
+        expo = jnp.exp2((s[rows, :] - top) * to_exp2)
+        total += jnp.sum(expo, axis=0, keepdims=True)
+        expo = expo.astype(jnp.bfloat16)
+        e[h, rows, cols] = expo
+        attended += dot(vt[h, :, rows], expo)
+    scale = 1.0 / total
+    ot[h, :, cols] = attended
+    inv[h, :, cols] = scale
+    qt[h, :, cols] = (query.astype(jnp.float32).T * scale).astype(jnp.bfloat16)
+
+
+def mix_kernel(
+    terms, cot, parts, hq, hk, hv,
+    gh_out, dq_out, dk_out, dv_out, w_out,
+    comb, sib, z1, z2, cbuf, gh, keep, wrecv, shard,
+    q, k, v, do, kt, vt, s, e, ot, inv, qt, dot_t, dqt, g, back,
+    load_sem, sib_send, sib_recv, z_send, z_recv, rs_send, rs_recv, ag_send, ag_recv,
+    gh_send, gh_recv, gh_local, out_send, out_recv, out_local, store_sem,
+):
+    expert = lax.axis_index("expert")
+    seq = lax.axis_index("seq")
+    dp = lax.axis_index("dp")
+    z, core = lax.div(expert, 2), lax.rem(expert, 2)
+    far, near = lax.div(seq, 4), lax.rem(seq, 4)
+    z_a, z_b = flip(z), 3 - z
+    targets = [flip(z_b), z_a, z_b, z]
+    to_pair = {"expert": z * 2 + 1 - core}
+    to_a = {"expert": z_a * 2 + core}
+    to_b = {"expert": z_b * 2 + core}
+    hops = {
+        "xa": ({"seq": far * 4 + flip(near)}, lax.rem(lax.div(near, 2) + lax.rem(near, 2), 2)),
+        "xb": ({"seq": far * 4 + 3 - near}, lax.div(near, 2)),
+        "ya": ({"dp": 1 - dp}, lax.rem(far + dp, 2)),
+        "yb": ({"dp": 1 - dp, "seq": (1 - far) * 4 + near}, far),
+    }
+    orders = [
+        ("xa", "xb", "ya", "yb"), ("xb", "xa", "yb", "ya"),
+        ("ya", "yb", "xa", "xb"), ("yb", "ya", "xb", "xa"),
+    ]
+    enter([to_pair, to_a, to_b, hops["ya"][0], hops["yb"][0]] + seq_peers())
+
+    sizes = (768, 384, 192, 96)
+    lands = (0, 768, 1152, 1344)
+    send_at, keep_at = [], []
+    for p in range(4):
+        base, sent, kept = 0, [], []
+        for i in range(4):
+            bit = hops[orders[p][i]][1]
+            sent.append(base + (1 - bit) * sizes[i])
+            base = base + bit * sizes[i]
+            kept.append(base)
+        send_at.append(sent)
+        keep_at.append(kept)
+
+    def span(start, size):
+        return pl.ds(pl.multiple_of(start, 32), size)
+
+    def rs_copy(p, i):
+        if i == 0:
+            src = parts.at[span(p * 1536 + send_at[p][0], 768), :]
+        else:
+            src = keep.at[p, span(send_at[p][i] - keep_at[p][0], sizes[i]), :]
+        dst = wrecv.at[p, pl.ds(lands[i], sizes[i]), :]
+        return remote(src, dst, rs_send.at[p, i], rs_recv.at[p, i], hops[orders[p][i]][0])
+
+    def rs_step(i):
+        for p in range(4):
+            rs_copy(p, i - 1).wait_recv()
+            rows = sizes[i - 1]
+            at = keep_at[p][i - 1] - keep_at[p][0]
+            if i < 4:
+                add_rows(
+                    (keep.at[p], at, None),
+                    [(keep.at[p], at), (wrecv.at[p], lands[i - 1])], rows, 32,
+                )
+                rs_copy(p, i).start()
+            else:
+                add_rows(
+                    (shard.at[p], 0, 1.0 / 16.0),
+                    [(keep.at[p], at), (wrecv.at[p], lands[3])], rows, 32,
+                )
+
+    def ag_copy(p, i):
+        hop = orders[p][3 - i]
+        size = sizes[3 - i]
+        rows = span(p * 1536 + keep_at[p][3 - i], size)
+        src = shard.at[p] if i == 0 else w_out.at[rows, :]
+        return remote(src, w_out.at[rows, :], ag_send.at[p, i], ag_recv.at[p, i], hops[hop][0])
+
+    def store_shard(p):
+        rows = span(p * 1536 + keep_at[p][3], 96)
+        return pltpu.make_async_copy(shard.at[p], w_out.at[rows, :], store_sem.at[1 + p])
+
+    def ag_step(i):
+        for p in range(4):
+            if i == 1:
+                store_shard(p).wait()
+            if i > 0:
+                ag_copy(p, i - 1).wait_recv()
+            if i < 4:
+                ag_copy(p, i).start()
+
+    sib_copies = []
+    for i in range(4):
+        copy = remote(
+            terms.at[targets[i] * 2 + 1 - core], sib.at[i], sib_send.at[i], sib_recv.at[i], to_pair
+        )
+        copy.start()
+        sib_copies.append(copy)
+    for p in range(4):
+        rs_copy(p, 0).start()
+    comb_loads = [
+        pltpu.make_async_copy(terms.at[targets[i] * 2 + core], comb.at[i], load_sem.at[i])
+        for i in range(4)
+    ]
+    keep_loads = [
+        pltpu.make_async_copy(
+            parts.at[span(p * 1536 + keep_at[p][0], 768), :], keep.at[p], load_sem.at[4 + p]
+        )
+        for p in range(4)
+    ]
+    cot_load = pltpu.make_async_copy(cot, cbuf, load_sem.at[8])
+    head_loads = []
+    for n, (src, dst) in enumerate(((hq, q), (hk, k), (hv, v))):
+        for h in range(2):
+            head_loads.append(
+                pltpu.make_async_copy(
+                    src.at[:, pl.ds(h * HD, HD)], dst.at[h], load_sem.at[9 + 2 * n + h]
+                )
+            )
+    for copy in comb_loads + head_loads + keep_loads + [cot_load]:
+        copy.start()
+
+    def z_copy(n):
+        first, second = pl.ds(0, 128), pl.ds(128, 128)
+        src, dst, target = (
+            (comb.at[0, first, :], z1.at[0, 0], to_a),
+            (comb.at[0, second, :], z1.at[1, 0], to_b),
+            (comb.at[1, first, :], z1.at[0, 1], to_a),
+            (comb.at[2, second, :], z1.at[1, 1], to_b),
+            (comb.at[2, first, :], z2.at[0], to_b),
+            (comb.at[1, second, :], z2.at[1], to_a),
+        )[n]
+        return remote(src, dst, z_send.at[n], z_recv.at[n], target)
+
+    def pair_sum(i, base, rows):
+        add_rows((comb.at[i], base, None), [(comb.at[i], base), (sib.at[i], base)], rows, 16)
+
+    def forward(first, last):
+        def body(index, carry):
+            forward_block(index, q, k, vt, s, e, ot, inv, qt)
+            return carry
+
+        lax.fori_loop(first, last, body, 0)
+
+    for copy in head_loads:
+        copy.wait()
+    for h in range(2):
+        kt[h] = k[h].T
+        vt[h] = v[h].T
+    for i in range(3):
+        comb_loads[i].wait()
+        sib_copies[i].wait_recv()
+        pair_sum(i, 0, 256)
+        if i == 0:
+            z_copy(0).start()
+            z_copy(1).start()
+        else:
+            z_copy(i + 1).start()
+    comb_loads[3].wait()
+    cot_load.wait()
+    sib_copies[3].wait_recv()
+    forward(0, 4)
+    for copy in keep_loads:
+        copy.wait()
+    rs_step(1)
+    forward(4, 6)
+    z_copy(0).wait_recv()
+    add_rows((comb.at[2], 0, None), [(comb.at[2], 0), (z1.at[0, 0], 0)], 128, 16)
+    z_copy(4).start()
+    z_copy(1).wait_recv()
+    add_rows((comb.at[1], 128, None), [(comb.at[1], 128), (z1.at[1, 0], 0)], 128, 16)
+    z_copy(5).start()
+    forward(6, 11)
+    rs_step(2)
+    forward(11, 13)
+    rs_step(3)
+    z_copy(2).wait_recv()
+    z_copy(3).wait_recv()
+    forward(13, 14)
+    rs_step(4)
+    for p in range(4):
+        store_shard(p).start()
+    ag_step(0)
+    forward(14, 16)
+    for p in range(2):
+        z_copy(4 + p).wait_recv()
+        add_rows(
+            (gh, 128 * p, None),
+            [(cbuf, 128 * p), (comb.at[3], 128 * p), (sib.at[3], 128 * p), (z1.at[p, 1], 0), (z2.at[p], 0)],
+            128, 16,
+        )
+    gh_copies = []
+    for d in range(1, 8):
+        to = lax.rem(seq + d, 8)
+        copy = remote(
+            gh.at[:, strip(to, 256)], do.at[strip(seq, 256), :], gh_send.at[d], gh_recv.at[d], {"seq": to}
+        )
+        copy.start()
+        gh_copies.append(copy)
+    copy = pltpu.make_async_copy(gh.at[:, strip(seq, 256)], do.at[strip(seq, 256), :], gh_local)
+    copy.start()
+    gh_copies.append(copy)
+    gh_store = pltpu.make_async_copy(gh, gh_out, store_sem.at[0])
+    gh_store.start()
+    ag_step(1)
+    for copy in gh_copies[:7]:
+        copy.wait_recv()
+    gh_copies[7].wait()
+    ag_step(2)
+
+    scale = HD ** -0.5
+    outs = (dq_out, dk_out, dv_out)
+
+    def out_copy(h, n, d):
+        to = lax.rem(seq + d, 8)
+        return remote(
+            back.at[n, h, strip(to, 256), :],
+            outs[n].at[:, pl.ds(pl.multiple_of(seq * 256 + h * HD, HD), HD)],
+            out_send.at[h, n, d],
+            out_recv.at[h, n, d],
+            {"seq": to},
+        )
+
+    def out_own(h, n):
+        return pltpu.make_async_copy(
+            back.at[n, h, strip(seq, 256), :],
+            outs[n].at[:, pl.ds(pl.multiple_of(seq * 256 + h * HD, HD), HD)],
+            out_local.at[h, n],
+        )
+
+    for h in range(2):
+        head = pl.ds(h * HD, HD)
+        norm = inv[h]
+        grad_t = do[:, head].astype(jnp.float32).T
+        delta = jnp.sum(grad_t * ot[h], axis=0, keepdims=True) * norm
+        dot_t[...] = (grad_t * norm).astype(jnp.bfloat16)
+        dqt[...] = jnp.zeros_like(dqt)
+
+        def chunk(d, carry):
+            at = lax.rem(seq + d, 8)
+            rows = strip(at, 256)
+            expo = e[h, rows, :]
+            grad_probs = dot_nt(v[h, rows, :], do[:, head])
+            g[...] = (expo.astype(jnp.float32) * (grad_probs - delta)).astype(jnp.bfloat16)
+            back[2, h, rows, :] = dot_nt(expo, dot_t[...]).astype(jnp.bfloat16)
+            back[1, h, rows, :] = (dot_nt(g[...], qt[h]) * scale).astype(jnp.bfloat16)
+            dqt[...] += dot(kt[h, :, rows], g[...])
+
+            @pl.when(d > 0)
+            def _():
+                out_copy(h, 1, d).start()
+                out_copy(h, 2, d).start()
+
+            return carry
+
+        lax.fori_loop(0, 4, chunk, 0)
+        if h == 0:
+            ag_step(3)
+        lax.fori_loop(4, 8, chunk, 0)
+        back[0, h] = (dqt[...] * (norm * scale)).T.astype(jnp.bfloat16)
+        for d in range(1, 8):
+            out_copy(h, 0, d).start()
+        for n in range(3):
+            out_own(h, n).start()
+    ag_step(4)
+
+    for copy in sib_copies + gh_copies[:7]:
+        copy.wait_send()
+    for n in range(6):
+        z_copy(n).wait_send()
+    for p in range(4):
+        for i in range(4):
+            rs_copy(p, i).wait_send()
+            ag_copy(p, i).wait_send()
+    gh_store.wait()
+    for h in range(2):
+        for n in range(3):
+            out_own(h, n).wait()
+            for d in range(1, 8):
+                out_copy(h, n, d).wait()
+
+
+def mix(terms, cot, parts, head_q, head_k, head_v):
+    dma = pltpu.SemaphoreType.DMA
+    bf16, f32 = jnp.bfloat16, jnp.float32
+    shapes = [(256, 2048)] * 4 + [(6144, 512)]
+    return pl.pallas_call(
+        mix_kernel,
+        out_shape=[jax.ShapeDtypeStruct(shape, bf16) for shape in shapes],
+        in_specs=[ANY] * 6,
+        out_specs=[ANY] * 5,
+        scratch_shapes=[
+            pltpu.VMEM((4, 256, 2048), bf16),
+            pltpu.VMEM((4, 256, 2048), bf16),
+            pltpu.VMEM((2, 2, 128, 2048), bf16),
+            pltpu.VMEM((2, 128, 2048), bf16),
+            pltpu.VMEM((256, 2048), bf16),
+            pltpu.VMEM((256, 2048), bf16),
+            pltpu.VMEM((4, 768, 512), bf16),
+            pltpu.VMEM((4, 1440, 512), bf16),
+            pltpu.VMEM((4, 96, 512), bf16),
+            pltpu.VMEM((2, 2048, HD), bf16),
+            pltpu.VMEM((2, 2048, HD), bf16),
+            pltpu.VMEM((2, 2048, HD), bf16),
+            pltpu.VMEM((2048, 256), bf16),
+            pltpu.VMEM((2, HD, 2048), bf16),
+            pltpu.VMEM((2, HD, 2048), bf16),
+            pltpu.VMEM((2048, 256), f32),
+            pltpu.VMEM((2, 2048, 2048), bf16),
+            pltpu.VMEM((2, HD, 2048), f32),
+            pltpu.VMEM((2, 1, 2048), f32),
+            pltpu.VMEM((2, HD, 2048), bf16),
+            pltpu.VMEM((HD, 2048), bf16),
+            pltpu.VMEM((HD, 2048), f32),
+            pltpu.VMEM((256, 2048), bf16),
+            pltpu.VMEM((3, 2, 2048, HD), bf16),
+            dma((15,)), dma((4,)), dma((4,)), dma((6,)), dma((6,)),
+            dma((4, 4)), dma((4, 4)), dma((4, 4)), dma((4, 4)),
+            dma((8,)), dma((8,)), dma, dma((2, 3, 8)), dma((2, 3, 8)), dma((2, 3)), dma((5,)),
+        ],
+        compiler_params=pltpu.CompilerParams(
+            collective_id=2, has_side_effects=True, vmem_limit_bytes=62 << 20
+        ),
+        name="mix",
+    )(terms, cot, parts, head_q, head_k, head_v)
+
+
 def expert_backward(rows_in, scaled_grad, gate_matrix, up_matrix, down_matrix):
     first = (((0,), (0,)), ((), ()))
     gate_value = dot(rows_in, gate_matrix)
@@ -358,18 +603,15 @@
     scaled_grad = jnp.einsum("bst,btd->bsd", pick_weight, all_c).reshape(-1, width)
     hidden_part, parts = expert_backward(rows_in, scaled_grad, w_gate[0], w_up[0], w_down[0])
     terms = jnp.einsum("bst,bsd->btd", pick, hidden_part.reshape(8, 128, width))
-    routed_sum = lax.psum_scatter(
-        terms.reshape(experts * rows, width), "expert", scatter_dimension=0, tiled=True
-    ).astype(jnp.float32)
-    grad_hidden = (cotangent.astype(jnp.float32) + routed_sum).astype(jnp.bfloat16)
-    sums = [lax.psum(part, ("dp", "seq")).astype(jnp.float32) for part in parts]
-    groups = jnp.float32(lax.axis_size("dp") * lax.axis_size("seq"))
-    grads = [(total / groups)[None].astype(jnp.bfloat16) for total in sums]
-    (head_grad,) = swap(start_to_heads, [grad_hidden], (2048, 256), 2, "grad_to_heads")
-    backs = attention(head_q, head_k, head_v, head_grad)
-    grad_query, grad_key, grad_value = swap(
-        start_to_tokens, backs, (rows, width), 3, "grads_to_tokens"
+    gate_part, up_part, down_part = parts
+    down_rows = jnp.swapaxes(down_part.reshape(512, 4, 512), 0, 1).reshape(2048, 512)
+    joined = jnp.concatenate([gate_part, up_part, down_rows], axis=0)
+    grad_hidden, grad_query, grad_key, grad_value, sums = mix(
+        terms, cotangent, joined, head_q, head_k, head_v
     )
+    grad_gate, grad_up = sums[:2048], sums[2048:4096]
+    grad_down = jnp.swapaxes(sums[4096:].reshape(4, 512, 512), 0, 1).reshape(512, 2048)
+    grads = [grad[None] for grad in (grad_gate, grad_up, grad_down)]
     return (grad_hidden, grad_query, grad_key, grad_value, *grads)
 
 

time: 372 us -> 287 us (0.77); the launches traced: 372 us -> 283 us
  waiting for transfers between devices: 111 us -> 0 us
  Pallas kernels: 186 us -> 213 us
  between operations: 15.8 us -> 1.08 us
  other arithmetic: 12.8 us -> 21.1 us
  local copies, waits for them, and re-layouts: 8.82 us -> 15.8 us
  matrix products: 37.1 us -> 31.9 us
    psum x1 -> x0, waiting for transfers between devices: 111 us -> none  [shards(): sums = [lax.psum(part, ('dp', 'seq')).astype(jnp.float32) for part in parts]]
    pallas_call x3 -> x1, Pallas kernels: 104 us -> 131 us  [mix(): pl.pallas_call(mix_kernel, out_shape=[jax.ShapeDtypeStruct(shape, bf16) f...]
    concatenate x0 -> x1, other arithmetic: none -> 17.5 us  [shards(): joined = jnp.concatenate([gate_part, up_part, down_rows], axis=0)]
    convert_element_type x3 -> x0, other arithmetic: 9.15 us -> none  [the longest x2 6.47 us: shards(): grads = [(total / groups)[None].astype(jnp.bfloat16) for total in sums]]
    slice x1 -> x2, local copies, waits for them, and re-layouts: 0.21 us -> 5.49 us  [the longest x1 5.27 us: shards(): sums[4096:].reshape(4, 512, 512)]
    dot_general x3, matrix products: 11.5 us -> 7.75 us  [expert_backward(): lax.dot_general(a, b, first, preferred_element_type=jnp.float32)]
    unnamed x41 -> x22, local copies, waits for them, and re-layouts: 8.6 us -> 5.76 us
  transfers between devices with their start and end apart: 2 -> 0, of which waited for: 1 -> 0; matrix products, arithmetic and copies ran while one was open for 5% -> 0% of each run, Pallas kernels for 0% -> 0%
where the time goes in v2:
time: 287 us; the launch traced here: 283 us
  Pallas kernels  213 us (74%)
  matrix products  31.9 us (11%)
  other arithmetic  21.1 us (7%)
  local copies, waits for them, and re-layouts  15.8 us (6%)
    pallas_call x1, Pallas kernels, mix(): pl.pallas_call(mix_kernel, out_shape=[jax.ShapeDtypeStruct(shape, bf16) f...  131 us
    pallas_call x1, Pallas kernels, spread(): pl.pallas_call(spread_kernel, out_shape=[jax.ShapeDtypeStruct(s, t) for s...  82 us
    concatenate x1, other arithmetic, shards(): joined = jnp.concatenate([gate_part, up_part, down_rows], axis=0)  17.5 us
    dot_general x3, matrix products, dot_nt(): return lax.dot_general(a, b, NT, preferred_element_type=jnp.float32)  7.77 us
    dot_general x3, matrix products, expert_backward(): lax.dot_general(a, b, first, preferred_element_type=jnp.float32)  7.75 us
    unnamed x22, local copies, waits for them, and re-layouts  5.76 us

profile of v2, /device:TPU:6, one launch (start us, length us, event | category | flops | bytes accessed | tf_op | source)
XLA Modules:
  0.0 282.6 jit_solution(12976166541811666333)
XLA Ops:
  0.6 0.7 convert_bitcast_fusion
  1.3 1.3 select_reduce_fusion.t_ref
  2.6 82.0 %spread.1 = (bf16[8,256,2048]{2,1,0:T(8,128)(2,1)}, bf16[8,256,2048]{2,1,0:T(8,128)(2,1)}, f32[8,8,256]{2,1,0:T(8,128)}, bf16[2048,256]{1,0:T(8,128)(2,1)}, bf16...) custom-call(bf16[256,2048]{1,0:T(8,128)(2,1)} %x_ref.1, bf16[256,2048]{1,0:T(8,128)(2,1)} %cot.1, ...), custom_call_target="tpu_custom_call" | custom-call | tf_op jit(solution)/shard_map/spread/pallas_call | solution.py:170
  84.6 0.9 broadcast_compare_fusion
  85.5 0.6 reduce-window.6
  86.1 0.2 slice_reduce_fusion
  86.3 0.1 add_bitcast_fusion
  86.4 0.0 copy-start
  86.4 4.6 %fusion.15 = bf16[8,128,2048]{2,1,0:T(8,128)(2,1)S(1)} fusion(bf16[8,256,2048]{2,1,0:T(8,128)(2,1)} %get-tuple-element.19, bf16[8,256]{1,0:T(8,128)(2,1)S(1)} %bitcast.70, s32[8,256]{1,0:T(8,128)S(1)} %add_bitcast_fusion, pred[8,256]{1,0:T(8,128)(4,1)S(1)} %bitcast.67), kind=kOutput, calls=%fused_computation.27 | convolution fusion | flops 1074528256 | bytes 12597248 | tf_op jit(solution)/shard_map/bst,btd->bsd/dot_general | solution.py:603
  91.1 1.2 copy-done
  92.3 0.0 copy-start.6
  92.3 2.5 fusion.13
  94.8 0.0 copy-done.6
  94.8 0.0 copy-start.7
  94.8 2.3 fusion.2
  97.1 0.0 copy-done.7
  97.1 2.3 fusion.5
  99.5 0.0 copy-start.5
  99.5 2.6 convolution_convert_fusion
  102.1 0.0 copy-done.5
  102.1 3.0 %multiply_convert_fusion.1 = (bf16[1024,512]{1,0:T(8,128)(2,1)S(1)}, bf16[1024,512]{1,0:T(8,128)(2,1)S(1)}) fusion(f32[1024,512]{1,0:T(8,128)S(1)} %fusion.2, f32[1024,512]{1,0:T(8,128)S(1)} %fusion.5, bf16[1024,2048]{1,0:T(8,128)(2,1)S(1)} %bitcast.65, bf16[1,512,2048]{2,1,0:T(8,128)(2,1)S(1)} %copy-done.5), kind=kOutput, calls=%fused_computation.18 | convolution fusion | flops 2154299392 | bytes 12582912 | tf_op jit(solution)/shard_map/dot_general | solution.py:22
  105.2 0.2 copy.40
  105.4 2.5 convolution_convert_fusion.1
  107.8 2.7 convolution_convert_fusion.2
  110.5 17.5 %pad_maximum_fusion.parts = bf16[6144,512]{1,0:T(8,128)(2,1)} fusion(bf16[2048,512]{1,0:T(8,128)(2,1)S(1)} %bitcast.58, bf16[2048,512]{1,0:T(8,128)(2,1)S(1)} %convolution_convert_fusion.1, bf16[2048,512]{1,0:T(8,128)(2,1)S(1)} %convolution_convert_fusion.2), kind=kLoop, calls=%fused_computation.1 | loop fusion | flops 18874368 | bytes 12582912 | tf_op jit(solution)/shard_map/concatenate | solution.py:608
  128.0 2.4 fusion
  130.4 2.4 add_convert_fusion
  132.8 4.6 %fusion.11.terms = bf16[8,256,2048]{2,1,0:T(8,128)(2,1)} fusion(bf16[8,128,2048]{2,1,0:T(8,128)(2,1)S(1)} %bitcast.57, s32[8,256]{1,0:T(8,128)S(1)} %add_bitcast_fusion, pred[8,256]{1,0:T(8,128)(4,1)S(1)} %bitcast.69), kind=kOutput, calls=%fused_computation.25 | convolution fusion | flops 1074266112 | bytes 12593152 | tf_op jit(solution)/shard_map/bst,bsd->btd/dot_general | solution.py:605
  137.4 130.8 %mix.1 = (bf16[256,2048]{1,0:T(8,128)(2,1)}, bf16[256,2048]{1,0:T(8,128)(2,1)}, bf16[256,2048]{1,0:T(8,128)(2,1)}, bf16[256,2048]{1,0:T(8,128)(2,1)}, bf16[6144,512]{1,0:T(8,128)(2,1)}) custom-call(bf16[8,256,2048]{2,1,0:T(8,128)(2,1)} %fusion.11.terms, bf16[256,2048]{1,0:T(8,128)(2,1)} %cot.1, bf16[6144,512]{1,0:T(8,128)(2,1)} %pad_maximum_fusion.parts, ...), custom_call_target="tpu_custom_call" | custom-call | tf_op jit(solution)/shard_map/mix/pallas_call | solution.py:515
  268.1 5.3 %fusion.28 = (bf16[2048,512]{1,0:T(8,128)(2,1)S(1)}, bf16[1,2048,512]{2,1,0:T(8,128)(2,1)}, bf16[1,2048,512]{2,1,0:T(8,128)(2,1)}) fusion(bf16[6144,512]{1,0:T(8,128)(2,1)} %get-tuple-element.28), kind=kLoop, calls=%fused_computation.48 | loop fusion | bytes 12582912 | tf_op jit(solution)/shard_map/slice | solution.py:613
  273.4 1.6 copy.31
  275.0 0.0 copy-start.4
  275.1 2.8 broadcast_in_dim_reshape.3
  277.8 0.0 copy-done.4
  277.8 0.0 copy-start.3
  277.8 0.0 copy-start.2
  277.8 1.0 copy.47
  278.8 0.6 copy-done.3
  279.4 0.0 copy-start.1
  279.4 1.0 copy.48
  280.4 0.0 copy-done.2
  280.4 1.0 copy.49
  281.4 0.0 copy-done.1
  281.4 1.0 copy.50
  (6 shorter events, 0.1 us)
Async XLA Ops:
  86.4 5.8 %copy-start = (bf16[8,256,2048]{2,1,0:T(8,128)(2,1)S(1)}, bf16[8,256,2048]{2,1,0:T(8,128)(2,1)}, u32[]{:S(2)}) copy-start(bf16[8,256,2048]{2,1,0:T(8,128)(2,1)} %get-tuple-element.20) | copy-start | bytes 25165828
  92.3 2.5 copy-start.6
  94.8 2.3 copy-start.7
  99.5 2.7 copy-start.5
  275.0 2.8 copy-start.4
  277.8 1.6 copy-start.3
  277.8 2.6 copy-start.2
  279.4 1.9 copy-start.1

commit v3 on v2

--- a/solution.py
+++ b/solution.py
@@ -82,10 +82,16 @@
     return index + 1 - 2 * lax.rem(index, 2)
 
 
-def spread_kernel(
-    x_ref, c_ref, t_ref, q_ref, k_ref, v_ref,
-    all_x, all_c, all_t, head_q, head_k, head_v,
-    send_sem, recv_sem, local_sem, t_send, t_recv, seq_send, seq_recv, seq_local,
+def dot_tn(a, b):
+    return lax.dot_general(a, b, (((0,), (0,)), ((), ())), preferred_element_type=jnp.float32)
+
+
+def experts_kernel(
+    x_ref, c_ref, t_ref, q_ref, k_ref, v_ref, wg_ref, wu_ref, wd_ref,
+    terms, parts, head_q, head_k, head_v,
+    all_x, all_c, all_t, wg, wu, wd, own_weight, own_rank, pick, pick_weight, pick_t,
+    rows_in, gate_value, up_value, scaled, inner, grad_gate, grad_up, hidden, stage, acc, joined,
+    send_sem, recv_sem, load_sem, t_send, t_recv, seq_send, seq_recv, seq_local, stage_sem, part_sem,
 ):
     me = lax.axis_index("expert")
     right, left, across = [lax.rem(me + d, 8) for d in (2, 6, 4)]
@@ -124,21 +130,115 @@
         small.append(copy)
     for a in (0, 1):
         for half in (0, 1):
+            send(a, half, me, True, pair, 3)
+        for half in (0, 1):
             send(a, half, me, True, right, 0)
             send(a, 1 - half, me, True, left, 1)
-        for half in (0, 1):
-            send(a, half, me, True, pair, 3)
-    local = [
-        pltpu.make_async_copy(x_ref, all_x.at[me], local_sem.at[0]),
-        pltpu.make_async_copy(c_ref, all_c.at[me], local_sem.at[1]),
-        pltpu.make_async_copy(t_ref, all_t.at[me], local_sem.at[2]),
+    loads = [
+        pltpu.make_async_copy(src, dst, load_sem.at[n])
+        for n, (src, dst) in enumerate((
+            (t_ref, all_t.at[me]), (x_ref, all_x.at[me]), (wg_ref.at[0], wg), (wu_ref.at[0], wu),
+            (c_ref, all_c.at[me]), (wd_ref.at[0], wd),
+        ))
     ]
-    for copy in local:
+    for copy in loads:
         copy.start()
     heads = start_to_heads(
         (q_ref, k_ref, v_ref), (head_q, head_k, head_v), seq_send, seq_recv, seq_local
     )
-    for a in (0, 1):
+
+    loads[0].wait()
+    for copy in small:
+        copy.wait_recv()
+    for b in range(8):
+        own_weight[pl.ds(b, 1), :] = all_t[b, pl.ds(me, 1), :]
+    before = lax.broadcasted_iota(jnp.int32, (256, 256), 0)
+    after = lax.broadcasted_iota(jnp.int32, (256, 256), 1)
+    upto = jnp.where(before <= after, 1.0, 0.0).astype(jnp.bfloat16)
+    taken = jnp.where(own_weight[...] > 0.0, 1.0, 0.0).astype(jnp.bfloat16)
+    own_rank[...] = dot(taken, upto) - 1.0
+
+    def fill_picks(b, carry):
+        weight = own_weight[pl.ds(b, 1), :]
+        rank = own_rank[pl.ds(b, 1), :]
+        slot = lax.broadcasted_iota(jnp.int32, (128, 256), 0).astype(jnp.float32)
+        hit = (slot == rank) & (weight > 0.0)
+        chosen = jnp.where(hit, 1.0, 0.0)
+        pick[b] = chosen.astype(jnp.bfloat16)
+        pick_weight[b] = jnp.where(hit, jnp.broadcast_to(weight, hit.shape), 0.0).astype(jnp.bfloat16)
+        pick_t[b] = chosen.T.astype(jnp.bfloat16)
+        return carry
+
+    lax.fori_loop(0, 8, fill_picks, 0)
+
+    def gather_rows(chooser, source, base, out):
+        for i in range(2):
+            block = base + i
+
+            @pl.loop(0, 2048, step=512)
+            def _(at):
+                cols = pl.ds(pl.multiple_of(at, 512), 512)
+                out[pl.ds(i * 128, 128), cols] = dot(chooser[block], source[block, :, cols]).astype(jnp.bfloat16)
+
+    def first_half(n, chip):
+        gather_rows(pick, all_x, chip * 2, rows_in.at[n])
+        gate_value[n] = dot(rows_in[n], wg[...])
+        up_value[n] = dot(rows_in[n], wu[...])
+
+    def stage_copy(i, chip):
+        return pltpu.make_async_copy(stage.at[i], terms.at[chip * 2 + i], stage_sem.at[i])
+
+    def second_half(n, chip, previous):
+        gather_rows(pick_weight, all_c, chip * 2, scaled)
+        grad_inner = dot_nt(scaled[...], wd[...])
+        gate, up = gate_value[n], up_value[n]
+        sig = jax.nn.sigmoid(gate)
+        active = gate * sig
+        inner[...] = (active * up).astype(jnp.bfloat16)
+        grad_gate[...] = (grad_inner * up * sig * (1.0 + gate * (1.0 - sig))).astype(jnp.bfloat16)
+        grad_up[...] = (grad_inner * active).astype(jnp.bfloat16)
+
+        @pl.loop(0, 2048, step=512)
+        def _(at):
+            cols = pl.ds(pl.multiple_of(at, 512), 512)
+            hidden[:, cols] = (
+                dot_nt(grad_gate[...], wg[cols, :]) + dot_nt(grad_up[...], wu[cols, :])
+            ).astype(jnp.bfloat16)
+
+        for i in range(2):
+            if previous is not None:
+                stage_copy(i, previous).wait()
+
+            @pl.loop(0, 2048, step=512)
+            def _(at):
+                cols = pl.ds(pl.multiple_of(at, 512), 512)
+                stage[i, :, cols] = dot(
+                    pick_t[chip * 2 + i], hidden[pl.ds(i * 128, 128), cols]
+                ).astype(jnp.bfloat16)
+
+            stage_copy(i, chip).start()
+
+        @pl.loop(0, 4)
+        def _(j):
+            cols = strip(j, 512)
+            for m, (a, b) in enumerate((
+                (rows_in.at[n, :, cols], grad_gate), (rows_in.at[n, :, cols], grad_up), (inner, scaled.at[:, cols]),
+            )):
+                rows = pl.ds(pl.multiple_of(m * 2048 + j * 512, 512), 512)
+                value = dot_tn(a[...], b[...])
+                if n == 0:
+                    acc[rows, :] = value
+                elif n < 3:
+                    acc[rows, :] += value
+                else:
+                    joined[rows, :] = (acc[rows, :] + value).astype(jnp.bfloat16)
+                    pltpu.make_async_copy(joined.at[rows, :], parts.at[rows, :], part_sem.at[m, j]).start()
+
+    def pair_arrived(a, kind, owner):
+        for half in (0, 1):
+            arrived(a, half, sibling(owner), kind)
+
+    def relay(a):
         arrived(a, 0, left, 0)
         send(a, 0, left, False, right, 2)
         send(a, 0, left, False, pair, 4)
@@ -149,35 +249,77 @@
         send(a, 1, left, False, pair, 4)
         arrived(a, 0, right, 1)
         send(a, 0, right, False, pair, 5)
-    for a in (0, 1):
+
+    def relay_last(a):
         for half in (0, 1):
             arrived(a, half, across, 2)
             send(a, half, across, False, pair, 6)
-    for a in (0, 1):
-        for half in (0, 1):
-            for kind, owner in ((3, me), (4, left), (5, right), (6, across)):
-                arrived(a, half, sibling(owner), kind)
-    for copy in sends:
+
+    chips = [lax.div(owner, 2) for owner in (me, left, right, across)]
+    loads[1].wait()
+    pair_arrived(0, 3, me)
+    loads[2].wait()
+    loads[3].wait()
+    first_half(0, chips[0])
+    loads[4].wait()
+    pair_arrived(1, 3, me)
+    loads[5].wait()
+    second_half(0, chips[0], None)
+    relay(0)
+    pair_arrived(0, 4, left)
+    first_half(1, chips[1])
+    pair_arrived(0, 5, right)
+    first_half(2, chips[2])
+    relay(1)
+    pair_arrived(1, 4, left)
+    second_half(1, chips[1], chips[0])
+    relay_last(0)
+    pair_arrived(1, 5, right)
+    second_half(2, chips[2], chips[1])
+    pair_arrived(0, 6, across)
+    first_half(3, chips[3])
+    relay_last(1)
+    pair_arrived(1, 6, across)
+    second_half(3, chips[3], chips[2])
+    for copy in sends + small:
         copy.wait_send()
-    for copy in local + small + heads:
+    for copy in heads:
         copy.wait()
-
-
-def spread(x, c, table, q, k, v):
-    shapes = [(8, 256, 2048)] * 2 + [(8, 8, 256)] + [(2048, 256)] * 3
-    types = [jnp.bfloat16] * 2 + [jnp.float32] + [jnp.bfloat16] * 3
+    for i in range(2):
+        stage_copy(i, chips[3]).wait()
+    for m in range(3):
+        for j in range(4):
+            rows = pl.ds(m * 2048 + j * 512, 512)
+            pltpu.make_async_copy(joined.at[rows, :], parts.at[rows, :], part_sem.at[m, j]).wait()
+
+
+def experts(x, c, table, q, k, v, w_gate, w_up, w_down):
     dma = pltpu.SemaphoreType.DMA
+    bf16, f32 = jnp.bfloat16, jnp.float32
+    shapes = [(8, 256, 2048), (6144, 512)] + [(2048, 256)] * 3
+    vmem = [
+        ((8, 256, 2048), bf16), ((8, 256, 2048), bf16), ((8, 8, 256), f32),
+        ((2048, 512), bf16), ((2048, 512), bf16), ((512, 2048), bf16),
+        ((8, 256), f32), ((8, 256), f32),
+        ((8, 128, 256), bf16), ((8, 128, 256), bf16), ((8, 256, 128), bf16),
+        ((4, 256, 2048), bf16), ((4, 256, 512), f32), ((4, 256, 512), f32),
+        ((256, 2048), bf16), ((256, 512), bf16), ((256, 512), bf16), ((256, 512), bf16),
+        ((256, 2048), bf16), ((2, 256, 2048), bf16), ((6144, 512), f32), ((6144, 512), bf16),
+    ]
     return pl.pallas_call(
-        spread_kernel,
-        out_shape=[jax.ShapeDtypeStruct(s, t) for s, t in zip(shapes, types)],
-        in_specs=[ANY] * 6,
-        out_specs=[ANY] * 6,
-        scratch_shapes=[
-            dma((28,)), dma((28,)), dma((3,)), dma((8,)), dma((8,)), dma((3, 8)), dma((3, 8)), dma((3,)),
+        experts_kernel,
+        out_shape=[jax.ShapeDtypeStruct(shape, bf16) for shape in shapes],
+        in_specs=[ANY] * 9,
+        out_specs=[ANY] * 5,
+        scratch_shapes=[pltpu.VMEM(*kind) for kind in vmem] + [
+            dma((28,)), dma((28,)), dma((6,)), dma((8,)), dma((8,)),
+            dma((3, 8)), dma((3, 8)), dma((3,)), dma((2,)), dma((3, 4)),
         ],
-        compiler_params=pltpu.CompilerParams(collective_id=1, has_side_effects=True),
-        name="spread",
-    )(x, c, table, q, k, v)
+        compiler_params=pltpu.CompilerParams(
+            collective_id=1, has_side_effects=True, vmem_limit_bytes=62 << 20
+        ),
+        name="experts",
+    )(x, c, table, q, k, v, w_gate, w_up, w_down)
 
 
 def add_rows(out, terms, rows, step):
@@ -553,59 +695,18 @@
     )(terms, cot, parts, head_q, head_k, head_v)
 
 
-def expert_backward(rows_in, scaled_grad, gate_matrix, up_matrix, down_matrix):
-    first = (((0,), (0,)), ((), ()))
-    gate_value = dot(rows_in, gate_matrix)
-    up_value = dot(rows_in, up_matrix)
-    sigmoid_gate = jax.nn.sigmoid(gate_value)
-    activated = gate_value * sigmoid_gate
-    inner_value = (activated * up_value).astype(jnp.bfloat16)
-    grad_inner = dot_nt(scaled_grad, down_matrix)
-    grad_gate_value = (
-        grad_inner * up_value * sigmoid_gate * (1.0 + gate_value * (1.0 - sigmoid_gate))
-    ).astype(jnp.bfloat16)
-    grad_up_value = (grad_inner * activated).astype(jnp.bfloat16)
-    hidden_part = dot_nt(grad_gate_value, gate_matrix) + dot_nt(grad_up_value, up_matrix)
-    parts = [
-        lax.dot_general(a, b, first, preferred_element_type=jnp.float32).astype(jnp.bfloat16)
-        for a, b in (
-            (rows_in, grad_gate_value),
-            (rows_in, grad_up_value),
-            (inner_value, scaled_grad),
-        )
-    ]
-    return hidden_part.astype(jnp.bfloat16), parts
-
-
 def shards(
     attn_query, attn_key, attn_value, moe_input, cotangent,
     routes, route_weight, w_gate, w_up, w_down,
 ):
-    rows, width = moe_input.shape
-    experts = lax.axis_size("expert")
-    mine = lax.axis_index("expert")
-    expert_ids = jnp.arange(experts, dtype=jnp.int32)
+    expert_ids = jnp.arange(8, dtype=jnp.int32)
     hits = routes.T[:, None, :] == expert_ids[None, :, None]
     table = jnp.sum(
         jnp.where(hits, route_weight.astype(jnp.float32).T[:, None, :], 0.0), axis=0
     )
-    all_x, all_c, all_t, head_q, head_k, head_v = spread(
-        moe_input, cotangent, table, attn_query, attn_key, attn_value
+    terms, joined, head_q, head_k, head_v = experts(
+        moe_input, cotangent, table, attn_query, attn_key, attn_value, w_gate, w_up, w_down
     )
-    own = lax.dynamic_slice_in_dim(all_t, mine, 1, 1)[:, 0]
-    taken = own > 0.0
-    rank = jnp.cumsum(taken.astype(jnp.int32), axis=1) - 1
-    slot_ids = jnp.arange(128, dtype=jnp.int32)
-    matched = (rank[:, None, :] == slot_ids[None, :, None]) & taken[:, None, :]
-    pick = matched.astype(jnp.bfloat16)
-    pick_weight = jnp.where(matched, own[:, None, :], 0.0).astype(jnp.bfloat16)
-    rows_in = jnp.einsum("bst,btd->bsd", pick, all_x).reshape(-1, width)
-    scaled_grad = jnp.einsum("bst,btd->bsd", pick_weight, all_c).reshape(-1, width)
-    hidden_part, parts = expert_backward(rows_in, scaled_grad, w_gate[0], w_up[0], w_down[0])
-    terms = jnp.einsum("bst,bsd->btd", pick, hidden_part.reshape(8, 128, width))
-    gate_part, up_part, down_part = parts
-    down_rows = jnp.swapaxes(down_part.reshape(512, 4, 512), 0, 1).reshape(2048, 512)
-    joined = jnp.concatenate([gate_part, up_part, down_rows], axis=0)
     grad_hidden, grad_query, grad_key, grad_value, sums = mix(
         terms, cotangent, joined, head_q, head_k, head_v
     )

time: 287 us -> 244 us (0.85)
  matrix products: 31.9 us -> 0 us
  other arithmetic: 21.1 us -> 1.97 us
  Pallas kernels: 213 us -> 223 us
    dot_general x11 -> x0, matrix products: 31.9 us -> none  [the longest x3 7.77 us: dot_nt(): return lax.dot_general(a, b, NT, preferred_element_type=jnp.float32)]
    concatenate x1 -> x0, other arithmetic: 17.5 us -> none  [shards(): joined = jnp.concatenate([gate_part, up_part, down_rows], axis=0)]
    pallas_call x1, Pallas kernels: 82 us -> 89.7 us  [experts(): pl.pallas_call(experts_kernel, out_shape=[jax.ShapeDtypeStruct(shape, bf1...]
    unnamed x22 -> x12, local copies, waits for them, and re-layouts: 5.76 us -> 4.52 us
where the time goes in v3:
time: 244 us; the launch traced here: 240 us
  Pallas kernels  223 us (91%)
  local copies, waits for them, and re-layouts  14.2 us (6%)
    pallas_call x1, Pallas kernels, mix(): pl.pallas_call(mix_kernel, out_shape=[jax.ShapeDtypeStruct(shape, bf16) f...  133 us
    pallas_call x1, Pallas kernels, experts(): pl.pallas_call(experts_kernel, out_shape=[jax.ShapeDtypeStruct(shape, bf1...  89.7 us
    slice x1, local copies, waits for them, and re-layouts, shards(): sums[4096:].reshape(4, 512, 512)  5.27 us

profile of v3, /device:TPU:6, one launch (start us, length us, event | category | flops | bytes accessed | tf_op | source)
XLA Modules:
  0.0 239.7 jit_solution(9455505260191861249)
XLA Ops:
  0.6 0.7 convert_bitcast_fusion
  1.3 1.3 select_reduce_fusion.t_ref
  2.6 89.7 %experts.1 = (bf16[8,256,2048]{2,1,0:T(8,128)(2,1)}, bf16[6144,512]{1,0:T(8,128)(2,1)}, bf16[2048,256]{1,0:T(8,128)(2,1)}, bf16[2048,256]{1,0:T(8,128)(2,1)}, bf16[2048,256]{1,0:T(8,128)(2,1)}) custom-call(bf16[256,2048]{1,0:T(8,128)(2,1)} %x_ref.1, bf16[256,2048]{1,0:T(8,128)(2,1)} %cot.1, f32[8,256]{1,0:T(8,128)} %select_reduce_fusion.t_ref, ...), custom_call_target="tpu_custom_call" | custom-call | tf_op jit(solution)/shard_map/experts/pallas_call | solution.py:309
  92.3 133.2 %mix.1 = (bf16[256,2048]{1,0:T(8,128)(2,1)}, bf16[256,2048]{1,0:T(8,128)(2,1)}, bf16[256,2048]{1,0:T(8,128)(2,1)}, bf16[256,2048]{1,0:T(8,128)(2,1)}, bf16[6144,512]{1,0:T(8,128)(2,1)}) custom-call(bf16[8,256,2048]{2,1,0:T(8,128)(2,1)} %get-tuple-element.17.terms, bf16[256,2048]{1,0:T(8,128)(2,1)} %cot.1, bf16[6144,512]{1,0:T(8,128)(2,1)} %get-tuple-element.18.parts, ...), custom_call_target="tpu_custom_call" | custom-call | tf_op jit(solution)/shard_map/mix/pallas_call | solution.py:657
  225.5 5.3 %fusion = (bf16[2048,512]{1,0:T(8,128)(2,1)S(1)}, bf16[1,2048,512]{2,1,0:T(8,128)(2,1)}, bf16[1,2048,512]{2,1,0:T(8,128)(2,1)}) fusion(bf16[6144,512]{1,0:T(8,128)(2,1)} %get-tuple-element.26), kind=kLoop, calls=%fused_computation.5 | loop fusion | bytes 12582912 | tf_op jit(solution)/shard_map/slice | solution.py:714
  230.8 1.6 copy.18
  232.4 0.0 copy-start.3
  232.4 2.8 %broadcast_in_dim_reshape.3 = bf16[1,512,2048]{2,1,0:T(8,128)(2,1)} reshape(bf16[512,4,512]{2,1,0:T(4,128)(2,1)S(1)} %copy.18) | data formatting | bytes 4194304 | tf_op jit(solution)/shard_map/broadcast_in_dim;reshape | solution.py:715
  235.2 0.0 copy-done.3
  235.2 0.0 copy-start.2
  235.2 0.0 copy-start.1
  235.2 1.0 copy.23
  236.1 0.6 copy-done.2
  236.8 0.0 copy-start
  236.8 1.0 copy.24
  237.7 0.0 copy-done.1
  237.7 1.0 copy.25
  238.7 0.0 copy-done
  238.7 1.0 copy.26
Async XLA Ops:
  232.4 2.8 %copy-start.3 = (bf16[256,2048]{1,0:T(8,128)(2,1)S(1)}, bf16[256,2048]{1,0:T(8,128)(2,1)}, u32[]{:S(2)}) copy-start(bf16[256,2048]{1,0:T(8,128)(2,1)} %get-tuple-element.37) | copy-start | bytes 3145732
  235.2 1.6 copy-start.2
  235.2 2.6 %copy-start.1 = (bf16[256,2048]{1,0:T(8,128)(2,1)S(1)}, bf16[256,2048]{1,0:T(8,128)(2,1)}, u32[]{:S(2)}) copy-start(bf16[256,2048]{1,0:T(8,128)(2,1)} %get-tuple-element.39) | copy-start | bytes 3145732
  236.8 1.9 copy-start

commit v4 on v1

v4 whole, which is shorter than its diff:
```python
import functools
import math

import jax
import jax.numpy as jnp
from jax import lax
from jax.experimental import pallas as pl
from jax.experimental.pallas import tpu as pltpu
from jax.sharding import PartitionSpec as P

TOP = 2

HD = 128
NT = (((1,), (1,)), ((), ()))


def dot(a, b):
    return jnp.dot(a, b, preferred_element_type=jnp.float32)


def dot_nt(a, b):
    return lax.dot_general(a, b, NT, preferred_element_type=jnp.float32)


MESH = pl.DeviceIdType.MESH
ANY = pl.BlockSpec(memory_space=pl.ANY)


def enter(targets):
    barrier = pltpu.get_barrier_semaphore()
    for target in targets:
        pl.semaphore_signal(barrier, inc=1, device_id=target, device_id_type=MESH)
    pl.semaphore_wait(barrier, len(targets))


def remote(src, dst, send_sem, recv_sem, target):
    return pltpu.make_async_remote_copy(
        src_ref=src,
        dst_ref=dst,
        send_sem=send_sem,
        recv_sem=recv_sem,
        device_id=target,
        device_id_type=MESH,
    )


def strip(index, size):
    return pl.ds(pl.multiple_of(index * size, size), size)


def start_to_heads(srcs, dsts, send_sem, recv_sem, local_sem):
    me = lax.axis_index("seq")
    copies = []
    for a, (src, dst) in enumerate(zip(srcs, dsts)):
        for d in range(1, 8):
            to = lax.rem(me + d, 8)
            copies.append(
                remote(
                    src.at[:, strip(to, 256)],
                    dst.at[strip(me, 256), :],
                    send_sem.at[a, d],
                    recv_sem.at[a, d],
                    {"seq": to},
                )
            )
            copies[-1].start()
        copies.append(
            pltpu.make_async_copy(
                src.at[:, strip(me, 256)], dst.at[strip(me, 256), :], local_sem.at[a]
            )
        )
        copies[-1].start()
    return copies


def seq_peers():
    me = lax.axis_index("seq")
    return [{"seq": lax.rem(me + d, 8)} for d in range(1, 8)]


def sibling(index):
    return index + 1 - 2 * lax.rem(index, 2)


def dot_tn(a, b):
    return lax.dot_general(a, b, (((0,), (0,)), ((), ())), preferred_element_type=jnp.float32)


def flip(index):
    return index + 1 - 2 * lax.rem(index, 2)


def add_rows(out, base, terms, rows, step=16):
    @pl.loop(0, rows, step=step)
    def _(at):
        total = None
        for ref, start in terms:
            value = ref[pl.ds(pl.multiple_of(start + at, step), step), :].astype(jnp.float32)
            total = value if total is None else total + value
        out[pl.ds(pl.multiple_of(base + at, step), step), :] = total.astype(jnp.bfloat16)


def layer_kernel(
    x_ref, c_ref, t_ref, q_ref, k_ref, v_ref, wg_ref, wu_ref, wd_ref,
    gh_out, dq_out, dk_out, dv_out, gate_out, up_out, down_out, head_q, head_k, head_v,
    tokens, all_t, wg, wu, wd, own_weight, own_rank, pick, pick_weight, pick_t,
    rows_in, values, scaled, inner, grad_gate, grad_up, hidden, stage, joined,
    sib, z1, z2, wrecv, shard, do, ot, inv, dot_t, dqt,
    send_sem, recv_sem, load_sem, t_send, t_recv, seq_send, seq_recv, seq_local,
    sib_send, sib_recv, z_send, z_recv, rs_send, rs_recv, ag_send, ag_recv,
    gh_send, gh_recv, gh_local, out_send, out_recv, out_local, store_sem, shard_sem,
):
    me = lax.axis_index("expert")
    seq = lax.axis_index("seq")
    dp = lax.axis_index("dp")
    z, core = lax.div(me, 2), lax.rem(me, 2)
    far, near = lax.div(seq, 4), lax.rem(seq, 4)
    right, left, across = [lax.rem(me + d, 8) for d in (2, 6, 4)]
    pair = sibling(me)
    z_a, z_b = flip(z), 3 - z
    to_pair = {"expert": pair}
    to_a = {"expert": z_a * 2 + core}
    to_b = {"expert": z_b * 2 + core}
    hops = {
        "xa": ({"seq": far * 4 + flip(near)}, lax.rem(lax.div(near, 2) + lax.rem(near, 2), 2)),
        "xb": ({"seq": far * 4 + 3 - near}, lax.div(near, 2)),
        "ya": ({"dp": 1 - dp}, lax.rem(far + dp, 2)),
        "yb": ({"dp": 1 - dp, "seq": (1 - far) * 4 + near}, far),
    }
    orders = [
        ("xa", "xb", "ya", "yb"), ("xb", "xa", "yb", "ya"),
        ("ya", "yb", "xa", "xb"), ("yb", "ya", "xb", "xa"),
    ]
    enter(
        [{"expert": lax.rem(me + d, 8)} for d in range(1, 8)]
        + seq_peers()
        + [hops["ya"][0], hops["yb"][0]]
    )
    srcs = (x_ref, c_ref)
    sends = []

    def piece(a, half, owner, mine, target, send_at, recv_at):
        rows = pl.ds(half * 128, 128)
        dst = tokens.at[a * 8 + owner, rows, :]
        src = srcs[a].at[rows, :] if mine else dst
        return remote(src, dst, send_sem.at[send_at], recv_sem.at[recv_at], {"expert": target})

    def recv_index(kind, a, half):
        return kind * 4 + a * 2 + half

    def send(a, half, owner, mine, target, kind):
        copy = piece(a, half, owner, mine, target, len(sends), recv_index(kind, a, half))
        copy.start()
        sends.append(copy)

    def arrived(a, half, owner, kind):
        piece(a, half, owner, False, me, 0, recv_index(kind, a, half)).wait_recv()

    small = []
    for d in range(1, 8):
        to = lax.rem(me + d, 8)
        copy = remote(t_ref, all_t.at[me], t_send.at[d], t_recv.at[d], {"expert": to})
        copy.start()
        small.append(copy)
    for a in (0, 1):
        for half in (0, 1):
            send(a, half, me, True, pair, 3)
        for half in (0, 1):
            send(a, half, me, True, right, 0)
            send(a, 1 - half, me, True, left, 1)
    loads = [
        pltpu.make_async_copy(src, dst, load_sem.at[n])
        for n, (src, dst) in enumerate((
            (t_ref, all_t.at[me]), (x_ref, tokens.at[me]), (wg_ref.at[0], wg), (wu_ref.at[0], wu),
            (c_ref, tokens.at[8 + me]), (wd_ref.at[0], wd),
        ))
    ]
    for copy in loads:
        copy.start()
    heads = start_to_heads(
        (q_ref, k_ref, v_ref), (head_q, head_k, head_v), seq_send, seq_recv, seq_local
    )

    loads[0].wait()
    for copy in small:
        copy.wait_recv()
    for b in range(8):
        own_weight[pl.ds(b, 1), :] = all_t[b, pl.ds(me, 1), :]
    before = lax.broadcasted_iota(jnp.int32, (256, 256), 0)
    after = lax.broadcasted_iota(jnp.int32, (256, 256), 1)
    upto = jnp.where(before <= after, 1.0, 0.0).astype(jnp.bfloat16)
    taken = jnp.where(own_weight[...] > 0.0, 1.0, 0.0).astype(jnp.bfloat16)
    own_rank[...] = dot(taken, upto) - 1.0

    def fill_picks(b, carry):
        weight = own_weight[pl.ds(b, 1), :]
        rank = own_rank[pl.ds(b, 1), :]
        slot = lax.broadcasted_iota(jnp.int32, (128, 256), 0).astype(jnp.float32)
        hit = (slot == rank) & (weight > 0.0)
        chosen = jnp.where(hit, 1.0, 0.0)
        pick[b] = chosen.astype(jnp.bfloat16)
        pick_weight[b] = jnp.where(hit, jnp.broadcast_to(weight, hit.shape), 0.0).astype(jnp.bfloat16)
        pick_t[b] = chosen.T.astype(jnp.bfloat16)
        return carry

    lax.fori_loop(0, 8, fill_picks, 0)

    sizes, lands = (8, 4, 2, 1), (0, 8, 12, 14)
    send_at, keep_at = [], []
    for p in range(4):
        base, sent, kept = 0, [], []
        for i in range(4):
            bit = hops[orders[p][i]][1]
            sent.append(base + (1 - bit) * sizes[i])
            base = base + bit * sizes[i]
            kept.append(base)
        send_at.append(sent)
        keep_at.append(kept)

    def rs_copy(p, i):
        return remote(
            joined.at[p, pl.ds(send_at[p][i], sizes[i])],
            wrecv.at[p, pl.ds(lands[i], sizes[i])],
            rs_send.at[p, i], rs_recv.at[p, i], hops[orders[p][i]][0],
        )

    def rs_step(i):
        for p in range(4):
            rs_copy(p, i - 1).wait_recv()
            at = keep_at[p][i - 1]
            if i < 4:
                def add(r, carry):
                    total = joined[p, at + r].astype(jnp.float32) + wrecv[p, lands[i - 1] + r].astype(jnp.float32)
                    joined[p, at + r] = total.astype(jnp.bfloat16)
                    return carry

                lax.fori_loop(0, sizes[i - 1], add, 0)
                rs_copy(p, i).start()
            else:
                total = joined[p, at].astype(jnp.float32) + wrecv[p, 14].astype(jnp.float32)
                shard[p] = (total * (1.0 / 16.0)).astype(jnp.bfloat16)

    def final_rows(p, i, m):
        start, rows = keep_at[p][3 - i] * 32, sizes[3 - i] * 32
        if m < 2:
            return (gate_out, up_out)[m].at[0, pl.ds(pl.multiple_of(p * 512 + start, 32), rows), :]
        return down_out.at[0, pl.ds(pl.multiple_of(start, 32), rows), pl.ds(p * 512, 512)]

    def ag_copy(p, i, m):
        dst = final_rows(p, i, m)
        src = shard.at[p, pl.ds(m * 32, 32), :] if i == 0 else dst
        return remote(src, dst, ag_send.at[p, i, m], ag_recv.at[p, i, m], hops[orders[p][3 - i]][0])

    def store_shard(p, m):
        return pltpu.make_async_copy(
            shard.at[p, pl.ds(m * 32, 32), :], final_rows(p, 0, m), shard_sem.at[p, m]
        )

    def ag_step(i):
        for p in range(4):
            for m in range(3):
                if i == 0:
                    store_shard(p, m).start()
                if i == 1:
                    store_shard(p, m).wait()
                if i > 0:
                    ag_copy(p, i - 1, m).wait_recv()
            for m in range(3):
                if i < 4:
                    ag_copy(p, i, m).start()

    def gather_rows(chooser, first, base, out):
        for i in range(2):
            block = base + i

            @pl.loop(0, 2048, step=512)
            def _(at):
                cols = pl.ds(pl.multiple_of(at, 512), 512)
                out[pl.ds(i * 128, 128), cols] = dot(
                    chooser[block], tokens[first + block, :, cols]
                ).astype(jnp.bfloat16)

    def first_half(n, chip):
        gather_rows(pick, 0, chip * 2, rows_in.at[n])
        values[n // 2 % 2 if n < 3 else 0, 0] = dot(rows_in[n], wg[...])
        values[n // 2 % 2 if n < 3 else 0, 1] = dot(rows_in[n], wu[...])

    def sib_copy(n):
        return remote(stage.at[n % 2], sib.at[n], sib_send.at[n], sib_recv.at[n], to_pair)

    def scatter_rows(chip, which, out):
        @pl.loop(0, 2048, step=512)
        def _(at):
            cols = pl.ds(pl.multiple_of(at, 512), 512)
            out[:, cols] = dot(
                pick_t[chip * 2 + which], hidden[pl.ds(pl.multiple_of(which * 128, 128), 128), cols]
            ).astype(jnp.bfloat16)

    def weight_part(n, j):
        cols = strip(j, 512)
        for m, (a, b) in enumerate((
            (rows_in.at[n, :, cols], grad_gate), (rows_in.at[n, :, cols], grad_up), (inner, scaled.at[:, cols]),
        )):
            rows = pl.ds(m * 32, 32)
            value = dot_tn(a[...], b[...]).reshape(16, 32, 512)
            if n > 0:
                value += joined[j, :, rows, :].astype(jnp.float32)
            joined[j, :, rows, :] = value.astype(jnp.bfloat16)

    def second_half(n, chip):
        gather_rows(pick_weight, 8, chip * 2, scaled)
        grad_inner = dot_nt(scaled[...], wd[...])
        slot = 1 if n == 2 else 0
        gate, up = values[slot, 0], values[slot, 1]
        sig = jax.nn.sigmoid(gate)
        active = gate * sig
        inner[...] = (active * up).astype(jnp.bfloat16)
        grad_gate[...] = (grad_inner * up * sig * (1.0 + gate * (1.0 - sig))).astype(jnp.bfloat16)
        grad_up[...] = (grad_inner * active).astype(jnp.bfloat16)

        @pl.loop(0, 2048, step=512)
        def _(at):
            cols = pl.ds(pl.multiple_of(at, 512), 512)
            hidden[:, cols] = (
                dot_nt(grad_gate[...], wg[cols, :]) + dot_nt(grad_up[...], wu[cols, :])
            ).astype(jnp.bfloat16)

        if n >= 2:
            sib_copy(n - 2).wait_send()
        scatter_rows(chip, 1 - core, stage.at[n % 2])
        sib_copy(n).start()
        if n < 3:
            @pl.loop(0, 4)
            def _(j):
                weight_part(n, j)
        else:
            for j in range(4):
                weight_part(n, j)
                rs_copy(j, 0).start()
        scatter_rows(chip, core, rows_in.at[n])

    def pair_arrived(a, kind, owner):
        for half in (0, 1):
            arrived(a, half, sibling(owner), kind)

    def relay(a):
        arrived(a, 0, left, 0)
        send(a, 0, left, False, right, 2)
        send(a, 0, left, False, pair, 4)
        arrived(a, 1, right, 1)
        send(a, 1, right, False, left, 2)
        send(a, 1, right, False, pair, 5)
        arrived(a, 1, left, 0)
        send(a, 1, left, False, pair, 4)
        arrived(a, 0, right, 1)
        send(a, 0, right, False, pair, 5)

    def relay_last(a):
        for half in (0, 1):
            arrived(a, half, across, 2)
            send(a, half, across, False, pair, 6)

    def z_copy(n):
        first, second = pl.ds(0, 128), pl.ds(128, 128)
        src, dst, target = (
            (rows_in.at[3, first, :], z1.at[0, 0], to_a),
            (rows_in.at[3, second, :], z1.at[1, 0], to_b),
            (rows_in.at[1, first, :], z1.at[0, 1], to_a),
            (rows_in.at[2, second, :], z1.at[1, 1], to_b),
            (rows_in.at[2, first, :], z2.at[0], to_b),
            (rows_in.at[1, second, :], z2.at[1], to_a),
        )[n]
        return remote(src, dst, z_send.at[n], z_recv.at[n], target)

    def pair_sum(n):
        sib_copy(n).wait_recv()
        add_rows(rows_in.at[n], 0, [(rows_in.at[n], 0), (sib.at[n], 0)], 256)

    owner_a, owner_b = z_a * 2 + core, z_b * 2 + core
    kind_a = 5 - lax.rem(z, 2)
    kind_b = 9 - kind_a
    loads[1].wait()
    pair_arrived(0, 3, me)
    loads[2].wait()
    loads[3].wait()
    first_half(0, z)
    loads[4].wait()
    pair_arrived(1, 3, me)
    loads[5].wait()
    second_half(0, z)
    relay(0)
    pair_arrived(0, kind_a, owner_a)
    first_half(1, z_a)
    pair_arrived(0, kind_b, owner_b)
    first_half(2, z_b)
    relay(1)
    pair_arrived(1, kind_a, owner_a)
    second_half(1, z_a)
    relay_last(0)
    pair_arrived(1, kind_b, owner_b)
    second_half(2, z_b)
    pair_arrived(0, 6, across)
    first_half(3, lax.div(across, 2))
    pair_sum(1)
    z_copy(2).start()
    pair_sum(2)
    z_copy(3).start()
    relay_last(1)
    pair_arrived(1, 6, across)
    second_half(3, lax.div(across, 2))

    for copy in heads:
        copy.wait()
    head_loads = []
    for n, (src, dst, at) in enumerate(((head_q, wg, 0), (head_k, wg, 256), (head_v, wu, 0))):
        head_loads.append(
            pltpu.make_async_copy(src, dst.at[:, pl.ds(at, 256)], load_sem.at[6 + n])
        )
    cot_load = pltpu.make_async_copy(c_ref, scaled, load_sem.at[9])
    for copy in head_loads + [cot_load]:
        copy.start()
    pair_sum(3)
    z_copy(0).start()
    z_copy(1).start()
    for copy in sends + small:
        copy.wait_send()
    for copy in head_loads:
        copy.wait()

    def lanes(h):
        return pl.ds(pl.multiple_of(h * HD, HD), HD)

    def key_lanes(h):
        return pl.ds(pl.multiple_of(256 + h * HD, HD), HD)

    for h in range(2):
        wd[lanes(h), :] = wu[:, lanes(h)].T

    def forward_block(index, carry):
        h, at = lax.div(index, 8), lax.rem(index, 8)
        cols = strip(at, 256)
        to_exp2 = (HD ** -0.5) * math.log2(math.e)
        query = wg[cols, lanes(h)]
        top = None
        for i in range(8):
            score = dot_nt(wg[pl.ds(i * 256, 256), key_lanes(h)], query)
            values[i // 4, i // 2 % 2, :, pl.ds(i % 2 * 256, 256)] = score
            peak = jnp.max(score, axis=0, keepdims=True)
            top = peak if top is None else jnp.maximum(top, peak)
        total = jnp.zeros((1, 256), jnp.float32)
        attended = jnp.zeros((HD, 256), jnp.float32)
        for i in range(8):
            score = values[i // 4, i // 2 % 2, :, pl.ds(i % 2 * 256, 256)]
            expo = jnp.exp2((score - top) * to_exp2)
            total += jnp.sum(expo, axis=0, keepdims=True)
            expo = expo.astype(jnp.bfloat16)
            tokens[h * 8 + i, :, cols] = expo
            attended += dot(wd[lanes(h), pl.ds(i * 256, 256)], expo)
        scale = 1.0 / total
        ot[h, :, cols] = attended
        inv[h, :, cols] = scale
        wd[key_lanes(h), cols] = (query.astype(jnp.float32).T * scale).astype(jnp.bfloat16)
        return carry

    def forward(first, last):
        lax.fori_loop(first, last, forward_block, 0)

    forward(0, 6)
    rs_step(1)
    z_copy(0).wait_recv()
    add_rows(rows_in.at[2], 0, [(rows_in.at[2], 0), (z1.at[0, 0], 0)], 128)
    z_copy(4).start()
    z_copy(1).wait_recv()
    add_rows(rows_in.at[1], 128, [(rows_in.at[1], 128), (z1.at[1, 0], 0)], 128)
    z_copy(5).start()
    forward(6, 10)
    rs_step(2)
    forward(10, 12)
    rs_step(3)
    forward(12, 13)
    rs_step(4)
    ag_step(0)
    forward(13, 16)
    cot_load.wait()
    sib_copy(0).wait_recv()
    sib_copy(2).wait_send()
    gh = stage.at[0]
    for p in range(2):
        z_copy(2 + p).wait_recv()
        z_copy(4 + p).wait_recv()
        add_rows(
            gh, 128 * p,
            [
                (scaled, 128 * p), (rows_in.at[0], 128 * p), (sib.at[0], 128 * p),
                (z1.at[p, 1], 0), (z2.at[p], 0),
            ],
            128,
        )
    gh_copies = []
    for d in range(1, 8):
        to = lax.rem(seq + d, 8)
        copy = remote(
            gh.at[:, strip(to, 256)], do.at[strip(seq, 256), :], gh_send.at[d], gh_recv.at[d], {"seq": to}
        )
        copy.start()
        gh_copies.append(copy)
    gh_own = pltpu.make_async_copy(gh.at[:, strip(seq, 256)], do.at[strip(seq, 256), :], gh_local)
    gh_own.start()
    gh_store = pltpu.make_async_copy(gh, gh_out, store_sem)
    gh_store.start()
    ag_step(1)
    for h in range(2):
        wd[lanes(h), :] = wg[:, key_lanes(h)].T
    for copy in gh_copies:
        copy.wait_recv()
    gh_own.wait()
    ag_step(2)

    scale = HD ** -0.5
    outs = (dq_out, dk_out, dv_out)

    def back(n, h, rows):
        return (wg, wg, wu)[n].at[rows, key_lanes(h) if n == 1 else lanes(h)]

    def out_copy(h, n, d):
        to = lax.rem(seq + d, 8)
        return remote(
            back(n, h, strip(to, 256)), outs[n].at[:, lanes(seq * 2 + h)],
            out_send.at[h, n, d], out_recv.at[h, n, d], {"seq": to},
        )

    def out_own(h, n):
        return pltpu.make_async_copy(
            back(n, h, strip(seq, 256)), outs[n].at[:, lanes(seq * 2 + h)], out_local.at[h, n]
        )

    for h in range(2):
        head = pl.ds(h * HD, HD)
        norm = inv[h]
        grad_t = do[:, head].astype(jnp.float32).T
        delta = jnp.sum(grad_t * ot[h], axis=0, keepdims=True) * norm
        dot_t[...] = (grad_t * norm).astype(jnp.bfloat16)
        dqt[...] = jnp.zeros_like(dqt)

        def chunk(d, carry):
            at = lax.rem(seq + d, 8)
            rows = strip(at, 256)
            expo = tokens[h * 8 + at]
            grad_probs = dot_nt(wu[rows, head], do[:, head])
            hidden[...] = (expo.astype(jnp.float32) * (grad_probs - delta)).astype(jnp.bfloat16)
            wu[rows, head] = dot_nt(expo, dot_t[...]).astype(jnp.bfloat16)
            wg[rows, key_lanes(h)] = (dot_nt(hidden[...], wd[key_lanes(h), :]) * scale).astype(jnp.bfloat16)
            dqt[...] += dot(wd[lanes(h), rows], hidden[...])

            @pl.when(d > 0)
            def _():
                out_copy(h, 1, d).start()
                out_copy(h, 2, d).start()

            return carry

        lax.fori_loop(0, 4, chunk, 0)
        if h == 0:
            ag_step(3)
        lax.fori_loop(4, 8, chunk, 0)
        wg[:, head] = (dqt[...] * (norm * scale)).T.astype(jnp.bfloat16)
        for d in range(1, 8):
            out_copy(h, 0, d).start()
        for n in range(3):
            out_own(h, n).start()
    ag_step(4)

    sib_copy(3).wait_send()
    for copy in gh_copies:
        copy.wait_send()
    for n in range(6):
        z_copy(n).wait_send()
    for p in range(4):
        for i in range(4):
            rs_copy(p, i).wait_send()
            for m in range(3):
                ag_copy(p, i, m).wait_send()
    gh_store.wait()
    for h in range(2):
        for n in range(3):
            out_own(h, n).wait()
            for d in range(1, 8):
                out_copy(h, n, d).wait()


def layer(*arrays):
    dma = pltpu.SemaphoreType.DMA
    bf16, f32 = jnp.bfloat16, jnp.float32
    shapes = [(256, 2048)] * 4 + [(1, 2048, 512)] * 2 + [(1, 512, 2048)] + [(2048, 256)] * 3
    vmem = [
        ((16, 256, 2048), bf16), ((8, 8, 256), f32),
        ((2048, 512), bf16), ((2048, 512), bf16), ((512, 2048), bf16),
        ((8, 256), f32), ((8, 256), f32),
        ((8, 128, 256), bf16), ((8, 128, 256), bf16), ((8, 256, 128), bf16),
        ((4, 256, 2048), bf16), ((2, 2, 256, 512), f32),
        ((256, 2048), bf16), ((256, 512), bf16), ((256, 512), bf16), ((256, 512), bf16),
        ((256, 2048), bf16), ((2, 256, 2048), bf16), ((4, 16, 96, 512), bf16),
        ((4, 256, 2048), bf16), ((2, 2, 128, 2048), bf16), ((2, 128, 2048), bf16),
        ((4, 15, 96, 512), bf16), ((4, 96, 512), bf16), ((2048, 256), bf16),
        ((2, HD, 2048), f32), ((2, 1, 2048), f32), ((HD, 2048), bf16), ((HD, 2048), f32),
    ]
    sems = [
        (28,), (28,), (10,), (8,), (8,), (3, 8), (3, 8), (3,),
        (4,), (4,), (6,), (6,), (4, 4), (4, 4), (4, 4, 3), (4, 4, 3),
        (8,), (8,), (), (2, 3, 8), (2, 3, 8), (2, 3), (), (4, 3),
    ]
    return pl.pallas_call(
        layer_kernel,
        out_shape=[jax.ShapeDtypeStruct(shape, bf16) for shape in shapes],
        in_specs=[ANY] * len(arrays),
        out_specs=[ANY] * len(shapes),
        scratch_shapes=[pltpu.VMEM(*kind) for kind in vmem] + [dma(s) if s else dma for s in sems],
        compiler_params=pltpu.CompilerParams(
            collective_id=1, has_side_effects=True, vmem_limit_bytes=63 << 20
        ),
        name="layer",
    )(*arrays)


def shards(
    attn_query, attn_key, attn_value, moe_input, cotangent,
    routes, route_weight, w_gate, w_up, w_down,
):
    expert_ids = jnp.arange(8, dtype=jnp.int32)
    hits = routes.T[:, None, :] == expert_ids[None, :, None]
    table = jnp.sum(
        jnp.where(hits, route_weight.astype(jnp.float32).T[:, None, :], 0.0), axis=0
    )
    results = layer(
        moe_input, cotangent, table, attn_query, attn_key, attn_value, w_gate, w_up, w_down
    )
    return tuple(results[:7])


def solution(mesh):
    tokens = P(("dp", "expert", "seq"), None)
    weights = P("expert", None, None)
    return jax.shard_map(
        shards,
        mesh=mesh,
        in_specs=(tokens,) * 7 + (weights,) * 3,
        out_specs=(tokens,) * 4 + (weights,) * 3,
        check_vma=False,
    )
```

time: 372 us -> 233 us (0.63)
  waiting for transfers between devices: 111 us -> 0 us
  matrix products: 37.1 us -> 0 us
  Pallas kernels: 186 us -> 218 us
  between operations: 15.8 us -> 0.67 us
  other arithmetic: 12.8 us -> 1.97 us
    psum x1 -> x0, waiting for transfers between devices: 111 us -> none  [shards(): sums = [lax.psum(part, ('dp', 'seq')).astype(jnp.float32) for part in parts]]
    dot_general x11 -> x0, matrix products: 37.1 us -> none  [the longest x3 11.5 us: expert_backward(): lax.dot_general(a, b, first, preferred_element_type=jnp.float32)]
    pallas_call x4 -> x1, Pallas kernels: 186 us -> 218 us  [layer(): pl.pallas_call(layer_kernel, out_shape=[jax.ShapeDtypeStruct(shape, bf16)...]
    convert_element_type x4 -> x0, other arithmetic: 9.16 us -> none  [the longest x2 6.47 us: shards(): grads = [(total / groups)[None].astype(jnp.bfloat16) for total in sums]]
    unnamed x41 -> x19, local copies, waits for them, and re-layouts: 8.6 us -> 11.5 us
  transfers between devices with their start and end apart: 2 -> 0, of which waited for: 1 -> 0; matrix products, arithmetic and copies ran while one was open for 5% -> 0% of each run, Pallas kernels for 0% -> 0%
where the time goes in v4:
time: 233 us; the launch traced here: 232 us
  Pallas kernels  218 us (94%)
  local copies, waits for them, and re-layouts  11.5 us (5%)
    pallas_call x1, Pallas kernels, layer(): pl.pallas_call(layer_kernel, out_shape=[jax.ShapeDtypeStruct(shape, bf16)...  218 us
    unnamed x19, local copies, waits for them, and re-layouts  11.5 us

profile of v4, /device:TPU:6, one launch (start us, length us, event | category | flops | bytes accessed | tf_op | source)
XLA Modules:
  0.0 232.0 jit_solution(996385541886386628)
XLA Ops:
  0.6 0.7 convert_bitcast_fusion
  1.3 1.3 select_reduce_fusion.t_ref
  2.6 217.8 %layer.1 = (bf16[256,2048]{1,0:T(8,128)(2,1)}, bf16[256,2048]{1,0:T(8,128)(2,1)}, bf16[256,2048]{1,0:T(8,128)(2,1)}, bf16[256,2048]{1,0:T(8,128)(2,1)}, bf16[1,2...) custom-call(bf16[256,2048]{1,0:T(8,128)(2,1)} %x_ref.1, ...), custom_call_target="tpu_custom_call" | custom-call | tf_op jit(solution)/shard_map/layer/pallas_call | solution.py:612
  220.4 0.0 copy-start.5
  220.4 0.0 copy-start.4
  220.4 2.5 %copy.24 = bf16[256,2048]{1,0:T(8,128)(2,1)} copy(bf16[256,2048]{1,0:T(8,128)(2,1)} %get-tuple-element.28) | data formatting | bytes 2097152
  222.9 0.0 copy-done.5
  222.9 0.0 copy-start.3
  222.9 1.0 copy.25
  223.8 0.0 copy-done.4
  223.9 0.0 copy-start.2
  223.9 1.0 copy.26
  224.8 0.0 copy-done.3
  224.8 1.0 copy.27
  225.8 0.1 copy-done.2
  225.9 0.0 copy-start.1
  225.9 1.3 copy.28
  227.3 1.0 copy-done.1
  228.3 0.0 copy-start
  228.3 1.3 copy.29
  229.6 1.0 copy-done
  230.6 1.3 copy.30
Async XLA Ops:
  220.4 2.5 %copy-start.5 = (bf16[256,2048]{1,0:T(8,128)(2,1)S(1)}, bf16[256,2048]{1,0:T(8,128)(2,1)}, u32[]{:S(2)}) copy-start(bf16[256,2048]{1,0:T(8,128)(2,1)} %get-tuple-element.29) | copy-start | bytes 3145732
  220.4 3.4 %copy-start.4 = (bf16[256,2048]{1,0:T(8,128)(2,1)S(1)}, bf16[256,2048]{1,0:T(8,128)(2,1)}, u32[]{:S(2)}) copy-start(bf16[256,2048]{1,0:T(8,128)(2,1)} %get-tuple-element.30) | copy-start | bytes 3145732
  222.9 1.9 copy-start.3
  223.9 2.1 copy-start.2
  225.9 2.3 %copy-start.1 = (bf16[1,2048,512]{2,1,0:T(8,128)(2,1)S(1)}, bf16[1,2048,512]{2,1,0:T(8,128)(2,1)}, u32[]{:S(2)}) copy-start(bf16[1,2048,512]{2,1,0:T(8,128)(2,1)} %get-tuple-element.33) | copy-start | bytes 6291460
  228.3 2.3 %copy-start = (bf16[1,512,2048]{2,1,0:T(8,128)(2,1)S(1)}, bf16[1,512,2048]{2,1,0:T(8,128)(2,1)}, u32[]{:S(2)}) copy-start(bf16[1,512,2048]{2,1,0:T(8,128)(2,1)} %get-tuple-element.34) | copy-start | bytes 6291460

commit v5 on v4

--- a/solution.py
+++ b/solution.py
@@ -318,6 +318,11 @@
         grad_gate[...] = (grad_inner * up * sig * (1.0 + gate * (1.0 - sig))).astype(jnp.bfloat16)
         grad_up[...] = (grad_inner * active).astype(jnp.bfloat16)
 
+        if n == 3:
+            for j in range(4):
+                weight_part(n, j)
+                rs_copy(j, 0).start()
+
         @pl.loop(0, 2048, step=512)
         def _(at):
             cols = pl.ds(pl.multiple_of(at, 512), 512)
@@ -333,10 +338,7 @@
             @pl.loop(0, 4)
             def _(j):
                 weight_part(n, j)
-        else:
-            for j in range(4):
-                weight_part(n, j)
-                rs_copy(j, 0).start()
+
         scatter_rows(chip, core, rows_in.at[n])
 
     def pair_arrived(a, kind, owner):
@@ -402,10 +404,10 @@
     pair_arrived(0, 6, across)
     first_half(3, lax.div(across, 2))
     pair_sum(1)
+    pair_sum(2)
+    relay_last(1)
     z_copy(2).start()
-    pair_sum(2)
     z_copy(3).start()
-    relay_last(1)
     pair_arrived(1, 6, across)
     second_half(3, lax.div(across, 2))
 
@@ -475,12 +477,7 @@
     z_copy(5).start()
     forward(6, 10)
     rs_step(2)
-    forward(10, 12)
-    rs_step(3)
-    forward(12, 13)
-    rs_step(4)
-    ag_step(0)
-    forward(13, 16)
+    forward(10, 13)
     cot_load.wait()
     sib_copy(0).wait_recv()
     sib_copy(2).wait_send()
@@ -508,9 +505,13 @@
     gh_own.start()
     gh_store = pltpu.make_async_copy(gh, gh_out, store_sem)
     gh_store.start()
-    ag_step(1)
+    rs_step(3)
+    forward(13, 16)
+    rs_step(4)
+    ag_step(0)
     for h in range(2):
         wd[lanes(h), :] = wg[:, key_lanes(h)].T
+    ag_step(1)
     for copy in gh_copies:
         copy.wait_recv()
     gh_own.wait()
@@ -622,6 +623,35 @@
     )(*arrays)
 
 
+def finish_kernel(*refs):
+    count = (len(refs) - 2) // 3
+    srcs, dsts, bufs = refs[:count], refs[count : 2 * count], refs[2 * count : 3 * count]
+    read_sem, write_sem = refs[3 * count :]
+    reads = [pltpu.make_async_copy(src, buf, read_sem.at[n]) for n, (src, buf) in enumerate(zip(srcs, bufs))]
+    writes = [pltpu.make_async_copy(buf, dst, write_sem.at[n]) for n, (buf, dst) in enumerate(zip(bufs, dsts))]
+    for read in reads:
+        read.start()
+    for read, write in zip(reads, writes):
+        read.wait()
+        write.start()
+    for write in writes:
+        write.wait()
+
+
+def finish(arrays):
+    count = len(arrays)
+    return pl.pallas_call(
+        finish_kernel,
+        out_shape=[jax.ShapeDtypeStruct(a.shape, a.dtype) for a in arrays],
+        in_specs=[ANY] * count,
+        out_specs=[ANY] * count,
+        scratch_shapes=[pltpu.VMEM(a.shape, a.dtype) for a in arrays]
+        + [pltpu.SemaphoreType.DMA((count,)), pltpu.SemaphoreType.DMA((count,))],
+        compiler_params=pltpu.CompilerParams(vmem_limit_bytes=62 << 20),
+        name="finish",
+    )(*arrays)
+
+
 def shards(
     attn_query, attn_key, attn_value, moe_input, cotangent,
     routes, route_weight, w_gate, w_up, w_down,
@@ -634,7 +664,7 @@
     results = layer(
         moe_input, cotangent, table, attn_query, attn_key, attn_value, w_gate, w_up, w_down
     )
-    return tuple(results[:7])
+    return tuple(finish(results[:7]))
 
 
 def solution(mesh):

time: 233 us -> 224 us (0.961)
  local copies, waits for them, and re-layouts: 11.5 us -> 0 us
  Pallas kernels: 218 us -> 222 us
    unnamed x19 -> x0, local copies, waits for them, and re-layouts: 11.5 us -> none
    pallas_call x0 -> x1, Pallas kernels: none -> 7.46 us  [finish(): pl.pallas_call(finish_kernel, out_shape=[jax.ShapeDtypeStruct(a.shape, a....]
    pallas_call x1, Pallas kernels: 218 us -> 214 us  [layer(): pl.pallas_call(layer_kernel, out_shape=[jax.ShapeDtypeStruct(shape, bf16)...]
where the time goes in v5:
time: 224 us
  Pallas kernels  222 us (99%)
    pallas_call x1, Pallas kernels, layer(): pl.pallas_call(layer_kernel, out_shape=[jax.ShapeDtypeStruct(shape, bf16)...  214 us
    pallas_call x1, Pallas kernels, finish(): pl.pallas_call(finish_kernel, out_shape=[jax.ShapeDtypeStruct(a.shape, a....  7.46 us

profile of v5, /device:TPU:6, one launch (start us, length us, event | category | flops | bytes accessed | tf_op | source)
XLA Modules:
  0.0 224.3 jit_solution(12361241347095975736)
XLA Ops:
  0.6 0.7 convert_bitcast_fusion
  1.3 1.3 select_reduce_fusion.t_ref
  2.6 214.1 %layer.1 = (bf16[256,2048]{1,0:T(8,128)(2,1)}, bf16[256,2048]{1,0:T(8,128)(2,1)}, bf16[256,2048]{1,0:T(8,128)(2,1)}, bf16[256,2048]{1,0:T(8,128)(2,1)}, bf16[1,2...) custom-call(bf16[256,2048]{1,0:T(8,128)(2,1)} %x_ref.1, ...), custom_call_target="tpu_custom_call" | custom-call | tf_op jit(solution)/shard_map/layer/pallas_call | solution.py:613
  216.7 7.5 %finish.1 = (bf16[256,2048]{1,0:T(8,128)(2,1)}, bf16[256,2048]{1,0:T(8,128)(2,1)}, bf16[256,2048]{1,0:T(8,128)(2,1)}, bf16[256,2048]{1,0:T(8,128)(2,1)}, bf16[1,...) custom-call(bf16[256,2048]{1,0:T(8,128)(2,1)} %get-tuple-element.14.refs_0_, ...), custom_call_target="tpu_custom_call" | custom-call | tf_op jit(solution)/shard_map/finish/pallas_call | solution.py:643

commit v6 on v5

--- a/solution.py
+++ b/solution.py
@@ -478,6 +478,9 @@
     forward(6, 10)
     rs_step(2)
     forward(10, 13)
+    rs_step(3)
+    rs_step(4)
+    ag_step(0)
     cot_load.wait()
     sib_copy(0).wait_recv()
     sib_copy(2).wait_send()
@@ -505,17 +508,15 @@
     gh_own.start()
     gh_store = pltpu.make_async_copy(gh, gh_out, store_sem)
     gh_store.start()
-    rs_step(3)
+    ag_step(1)
     forward(13, 16)
-    rs_step(4)
-    ag_step(0)
+    ag_step(2)
     for h in range(2):
         wd[lanes(h), :] = wg[:, key_lanes(h)].T
-    ag_step(1)
     for copy in gh_copies:
         copy.wait_recv()
     gh_own.wait()
-    ag_step(2)
+    ag_step(3)
 
     scale = HD ** -0.5
     outs = (dq_out, dk_out, dv_out)
@@ -561,8 +562,6 @@
             return carry
 
         lax.fori_loop(0, 4, chunk, 0)
-        if h == 0:
-            ag_step(3)
         lax.fori_loop(4, 8, chunk, 0)
         wg[:, head] = (dqt[...] * (norm * scale)).T.astype(jnp.bfloat16)
         for d in range(1, 8):

time: 224 us -> 223 us (level)
  Pallas kernels: 222 us -> 219 us
where the time goes in v6:
time: 223 us; the launch traced here: 222 us
  Pallas kernels  219 us (98%)
    pallas_call x1, Pallas kernels, layer(): pl.pallas_call(layer_kernel, out_shape=[jax.ShapeDtypeStruct(shape, bf16)...  212 us
    pallas_call x1, Pallas kernels, finish(): pl.pallas_call(finish_kernel, out_shape=[jax.ShapeDtypeStruct(a.shape, a....  7.46 us

profile of v6, /device:TPU:6, one launch (start us, length us, event | category | flops | bytes accessed | tf_op | source)
XLA Modules:
  0.0 222.2 jit_solution(4831590608195007872)
XLA Ops:
  0.6 0.7 convert_bitcast_fusion
  1.3 1.3 select_reduce_fusion.t_ref
  2.6 212.0 %layer.1 = (bf16[256,2048]{1,0:T(8,128)(2,1)}, bf16[256,2048]{1,0:T(8,128)(2,1)}, bf16[256,2048]{1,0:T(8,128)(2,1)}, bf16[256,2048]{1,0:T(8,128)(2,1)}, bf16[1,2...) custom-call(bf16[256,2048]{1,0:T(8,128)(2,1)} %x_ref.1, ...), custom_call_target="tpu_custom_call" | custom-call | tf_op jit(solution)/shard_map/layer/pallas_call | solution.py:612
  214.6 7.5 %finish.1 = (bf16[256,2048]{1,0:T(8,128)(2,1)}, bf16[256,2048]{1,0:T(8,128)(2,1)}, bf16[256,2048]{1,0:T(8,128)(2,1)}, bf16[256,2048]{1,0:T(8,128)(2,1)}, bf16[1,...) custom-call(bf16[256,2048]{1,0:T(8,128)(2,1)} %get-tuple-element.14.refs_0_, ...), custom_call_target="tpu_custom_call" | custom-call | tf_op jit(solution)/shard_map/finish/pallas_call | solution.py:642
